TPU v7x, 512 devices: a whole 4x8x8 slice. The times are simulated.
512 devices in a mesh: pot: 128 (over z_lo, y, x, core), grid: 4 (over z_hi).
Axes of the slice: x: 4, y: 8, z: 8 (z_hi: 4, z_lo: 2; z = z_hi * 2 + z_lo), core: 2. Of those that a mesh axis runs over, the one named last changes fastest.
Arguments:
- potentials: float32 [128, 32, 4096], P('pot', 'grid'), may hold values from -24 to 24
- orbitals: bfloat16 [32, 32, 4096], P(None, 'grid', 'pot'), may hold values from -0.5 to 2
- energies: float32 [32], replicated, may hold values from -2 to -0.2
- local_potential: float32 [32, 4096], replicated, may hold values from 0 to 3
- inverse_factor: bfloat16 [128, 128], replicated, may hold values from -8 to 8, as said below
Outputs:
- updated: float32 [128, 32, 4096], P('pot', 'grid')
- margins: float32 [128, 128], P('pot')
Inputs may be any that keep to these rules, and one draw needn't show every extreme that they name: `inverse_factor`: lower triangular with a positive diagonal.
All inputs are finite; a program needn't handle non-finite values.
Results may differ from a plain program's by a relative error of at most 0.0029.
Values may be sent and summed in bfloat16 or wider, within the bound.
A program may use at most 64 MiB of HBM per device.

v0:
```python
import jax
import jax.numpy as jnp
from jax import lax
from jax.sharding import PartitionSpec as P

NX = 64
NY = 64
NZ = 32
ORBITALS = 32
BLOCKS = 4
SWEEPS = 4


DAMPING = 0.8


def padded_2(block, sides, width):
    for axis, dim in sides:
        count = lax.axis_size(axis)
        forward = [(i, i + 1) for i in range(count - 1)]
        backward = [(target, source) for source, target in forward]
        low = lax.ppermute(
            lax.slice_in_dim(block, block.shape[dim] - width, None, axis=dim), axis, forward
        )
        high = lax.ppermute(lax.slice_in_dim(block, 0, width, axis=dim), axis, backward)
        block = jnp.concatenate([low, block, high], axis=dim)
    return block


def plane_neighbours(field, row_width):
    plane_size = field.shape[-1]
    widths = [(0, 0)] * (field.ndim - 1)
    padded = jnp.pad(field, widths + [(row_width, row_width)])
    along_y = padded[..., 2 * row_width :] + padded[..., :plane_size]
    column = jnp.arange(plane_size, dtype=jnp.int32) % row_width
    padded = jnp.pad(field, widths + [(1, 1)])
    right_side = jnp.where(column == row_width - 1, 0.0, padded[..., 2:])
    left_side = jnp.where(column == 0, 0.0, padded[..., :plane_size])
    return along_y + right_side + left_side


def across_slabs(answer):
    padded = padded_2(answer, (("grid", 2),), 1)
    return padded[:, :, 2:] + padded[:, :, :-2]


def absorb(orbital_block, energy_block, fields, local_here, along_planes):
    orbital = orbital_block.astype(jnp.float32)[:, None]
    diagonal = (3.0 + local_here[None] - energy_block[:, None, None])[:, None]
    source = -orbital * fields[None]
    answer = DAMPING * source / diagonal
    for sweep_index in range(SWEEPS - 1):
        nearby = along_planes(answer) + plane_neighbours(answer, NX)
        answer = answer + DAMPING * (source - diagonal * answer + 0.5 * nearby) / diagonal
    return jnp.sum(orbital * answer, axis=0)


def local(potentials, orbitals, energies, local_potential, inverse_factor):
    slab_depth = potentials.shape[1]
    grid_index = lax.axis_index("grid")
    local_here = lax.dynamic_slice_in_dim(local_potential, grid_index * slab_depth, slab_depth, 0)
    block_size = ORBITALS // BLOCKS
    response = jnp.zeros(potentials.shape, jnp.float32)
    for number in range(BLOCKS):
        orbital_block = orbitals[number * block_size : (number + 1) * block_size]
        gathered = lax.all_gather(orbital_block, "pot", axis=2, tiled=True)
        energy_block = energies[number * block_size : (number + 1) * block_size]
        response = response + absorb(gathered, energy_block, potentials, local_here, across_slabs)
    trial_block = (potentials + 4.0 / ORBITALS * response).astype(jnp.bfloat16)
    by_cells = lax.all_to_all(trial_block, "pot", split_axis=2, concat_axis=0, tiled=True)
    row_count = by_cells.shape[0]
    flattened = by_cells.reshape(row_count, -1)
    partial_margins = lax.dot_general(
        flattened, flattened, (((1,), (1,)), ((), ())), preferred_element_type=jnp.float32
    )
    combined = jnp.dot(inverse_factor, flattened, preferred_element_type=jnp.float32).reshape(
        by_cells.shape
    )
    updated = lax.all_to_all(combined, "pot", split_axis=0, concat_axis=2, tiled=True)
    own_count = potentials.shape[0]
    summed_all = lax.psum(partial_margins, ("pot", "grid"))
    own_rows = lax.dynamic_slice_in_dim(summed_all, lax.axis_index("pot") * own_count, own_count, 0)
    margins = own_rows / (NX * NY * NZ)
    return (updated, margins)


def solution(mesh):
    in_specs = (P("pot", "grid", None), P(None, "grid", "pot"), P(), P(), P())
    out_specs = (P("pot", "grid", None), P("pot", None))
    return jax.shard_map(local, mesh=mesh, in_specs=in_specs, out_specs=out_specs, check_vma=False)
```

profile of v0, /device:TPU:1, one launch (start us, length us, event | category | flops | bytes accessed | tf_op | source)
XLA Modules:
  0.0 1255.0 jit_solution(13859245160564547657)
XLA Ops:
  8.1 192.4 %all_gather.12 = bf16[8,8,4096]{1,0,2:T(8,128)(2,1)} all-gather(bf16[8,8,32]{1,0,2:T(8,128)(2,1)S(1)} %copy.397), channel_id=1, replica_groups=mesh['pot'=128,'grid'=4] {'pot'}, dimensions={2}, use_global_device_ids=true | all-gather | bytes 528384 | tf_op jit(solution)/shard_map/all_gather | solution.py:66
  200.4 7.9 copy.321
  208.4 184.1 %all_gather.13 = bf16[8,8,4096]{1,0,2:T(8,128)(2,1)} all-gather(bf16[8,8,32]{1,0,2:T(8,128)(2,1)S(1)} %copy.398), channel_id=1, replica_groups=mesh['pot'=128,'grid'=4] {'pot'}, dimensions={2}, use_global_device_ids=true | all-gather | bytes 528384 | tf_op jit(solution)/shard_map/all_gather | solution.py:66
  392.5 7.9 copy.338
  400.5 185.2 %all_gather.14 = bf16[8,8,4096]{1,0,2:T(8,128)(2,1)} all-gather(bf16[8,8,32]{1,0,2:T(8,128)(2,1)S(1)} %copy.399), channel_id=1, replica_groups=mesh['pot'=128,'grid'=4] {'pot'}, dimensions={2}, use_global_device_ids=true | all-gather | bytes 528384 | tf_op jit(solution)/shard_map/all_gather | solution.py:66
  585.7 7.9 copy.355
  593.7 184.1 %all_gather.15 = bf16[8,8,4096]{1,0,2:T(8,128)(2,1)} all-gather(bf16[8,8,32]{1,0,2:T(8,128)(2,1)S(1)} %copy.400), channel_id=1, replica_groups=mesh['pot'=128,'grid'=4] {'pot'}, dimensions={2}, use_global_device_ids=true | all-gather | bytes 528384 | tf_op jit(solution)/shard_map/all_gather | solution.py:66
  777.8 7.9 copy.372
  789.7 6.4 collective-permute-start.7
  797.6 6.7 collective-permute-start.1
  806.6 6.1 collective-permute-start.13
  816.3 6.1 collective-permute-start.19
  825.8 6.1 collective-permute-start.9
  835.3 6.1 collective-permute-start.3
  844.9 6.1 collective-permute-start.15
  854.5 6.1 collective-permute-start.21
  860.8 11.6 collective-permute-start.10
  874.5 6.1 collective-permute-start.11
  884.2 6.1 collective-permute-start.5
  894.0 6.1 collective-permute-start.17
  903.1 6.1 collective-permute-start.23
  918.1 22.4 %reduce.4 = bf16[4096,8]{1,0:T(8,128)(2,1)S(1)} reduce(bf16[4096,1,8]{2,1,0:T(2,128)(2,1)S(1)} %bitcast.279, bf16[]{:T(256)} %broadcast.208), dimensions={1}, to_apply=%bitcast.262.reduce_sub_computation | reduce | bytes 131074
  941.6 21.8 %all_to_all.33 = bf16[128,2,128]{2,1,0:T(2,128)(2,1)S(1)} all-to-all(bf16[128,2,128]{2,1,0:T(2,128)(2,1)S(1)} %reshape.105), channel_id=1, replica_groups=mesh['pot'=128,'grid'=4] {'pot'}, dimensions={0} | all-to-all | bytes 131072 | tf_op jit(solution)/shard_map/all_to_all | solution.py:70
  976.4 267.5 %all-reduce.26.cloned.1.call-done = f32[128,128]{1,0:T(8,128)} async-done(((f32[128,128]{1,0:T(8,128)}), f32[128,128]{1,0:T(8,128)}) %all-reduce.26.cloned.1.call-update) | async-done | bytes 65552 | tf_op jit(solution)/shard_map/psum | solution.py:81
  (142 shorter events, 64.8 us)
Async XLA Ops:
  788.3 18.2 %collective-permute-start.6 = (f32[8,1,1,4096]{3,0,2,1:T(8,128)S(1)}, f32[8,1,1,4096]{3,0,2,1:T(8,128)S(1)}, u32[]{:S(2)}, u32[]{:S(2)}) collective-permute-start(f32[8,1,1,4096]{3,0,2,1:T(8,128)S(1)} %copy.339), channel_id=1, source_target_pairs={{1,0},{2,1},{3,2},{5,4},{6,5},{7,6},{9,8},{10,9},{11,10},{13,12},{... | collective-permute-start | bytes 393224 | tf_op jit(solution)/shard_map/ppermute | solution.py:25
  789.7 23.1 %collective-permute-start.7 = (f32[8,1,1,4096]{3,0,2,1:T(8,128)S(1)}, f32[8,1,1,4096]{3,0,2,1:T(8,128)S(1)}, u32[]{:S(2)}, u32[]{:S(2)}) collective-permute-start(f32[8,1,1,4096]{3,0,2,1:T(8,128)S(1)} %copy.341), channel_id=1, source_target_pairs={{0,1},{1,2},{2,3},{4,5},{5,6},{6,7},{8,9},{9,10},{10,11},{12,13},{... | collective-permute-start | bytes 393224 | tf_op jit(solution)/shard_map/ppermute | solution.py:22
  796.3 20.0 %collective-permute-start = (f32[8,1,1,4096]{3,0,2,1:T(8,128)S(1)}, f32[8,1,1,4096]{3,0,2,1:T(8,128)S(1)}, u32[]{:S(2)}, u32[]{:S(2)}) collective-permute-start(f32[8,1,1,4096]{3,0,2,1:T(8,128)S(1)} %copy.322), channel_id=1, source_target_pairs={{1,0},{2,1},{3,2},{5,4},{6,5},{7,6},{9,8},{10,9},{11,10},{13,12},{... | collective-permute-start | bytes 393224 | tf_op jit(solution)/shard_map/ppermute | solution.py:25
  797.6 24.9 %collective-permute-start.1 = (f32[8,1,1,4096]{3,0,2,1:T(8,128)S(1)}, f32[8,1,1,4096]{3,0,2,1:T(8,128)S(1)}, u32[]{:S(2)}, u32[]{:S(2)}) collective-permute-start(f32[8,1,1,4096]{3,0,2,1:T(8,128)S(1)} %copy.324), channel_id=1, source_target_pairs={{0,1},{1,2},{2,3},{4,5},{5,6},{6,7},{8,9},{9,10},{10,11},{12,13},{... | collective-permute-start | bytes 393224 | tf_op jit(solution)/shard_map/ppermute | solution.py:22
  805.0 20.8 %collective-permute-start.12 = (f32[8,1,1,4096]{3,0,2,1:T(8,128)S(1)}, f32[8,1,1,4096]{3,0,2,1:T(8,128)S(1)}, u32[]{:S(2)}, u32[]{:S(2)}) collective-permute-start(f32[8,1,1,4096]{3,0,2,1:T(8,128)S(1)} %copy.356), channel_id=1, source_target_pairs={{1,0},{2,1},{3,2},{5,4},{6,5},{7,6},{9,8},{10,9},{11,10},{13,12},{... | collective-permute-start | bytes 393224 | tf_op jit(solution)/shard_map/ppermute | solution.py:25
  806.6 25.4 %collective-permute-start.13 = (f32[8,1,1,4096]{3,0,2,1:T(8,128)S(1)}, f32[8,1,1,4096]{3,0,2,1:T(8,128)S(1)}, u32[]{:S(2)}, u32[]{:S(2)}) collective-permute-start(f32[8,1,1,4096]{3,0,2,1:T(8,128)S(1)} %copy.358), channel_id=1, source_target_pairs={{0,1},{1,2},{2,3},{4,5},{5,6},{6,7},{8,9},{9,10},{10,11},{12,13},{... | collective-permute-start | bytes 393224 | tf_op jit(solution)/shard_map/ppermute | solution.py:22
  812.8 22.4 %collective-permute-start.18 = (f32[8,1,1,4096]{3,0,2,1:T(8,128)S(1)}, f32[8,1,1,4096]{3,0,2,1:T(8,128)S(1)}, u32[]{:S(2)}, u32[]{:S(2)}) collective-permute-start(f32[8,1,1,4096]{3,0,2,1:T(8,128)S(1)} %copy.373), channel_id=1, source_target_pairs={{1,0},{2,1},{3,2},{5,4},{6,5},{7,6},{9,8},{10,9},{11,10},{13,12},{... | collective-permute-start | bytes 393224 | tf_op jit(solution)/shard_map/ppermute | solution.py:25
  816.3 25.3 %collective-permute-start.19 = (f32[8,1,1,4096]{3,0,2,1:T(8,128)S(1)}, f32[8,1,1,4096]{3,0,2,1:T(8,128)S(1)}, u32[]{:S(2)}, u32[]{:S(2)}) collective-permute-start(f32[8,1,1,4096]{3,0,2,1:T(8,128)S(1)} %copy.375), channel_id=1, source_target_pairs={{0,1},{1,2},{2,3},{4,5},{5,6},{6,7},{8,9},{9,10},{10,11},{12,13},{... | collective-permute-start | bytes 393224 | tf_op jit(solution)/shard_map/ppermute | solution.py:22
  822.5 22.3 %collective-permute-start.8 = (f32[8,1,1,4096]{3,0,2,1:T(8,128)S(1)}, f32[8,1,1,4096]{3,0,2,1:T(8,128)S(1)}, u32[]{:S(2)}, u32[]{:S(2)}) collective-permute-start(f32[8,1,1,4096]{3,0,2,1:T(8,128)S(1)} %copy.344), channel_id=1, source_target_pairs={{1,0},{2,1},{3,2},{5,4},{6,5},{7,6},{9,8},{10,9},{11,10},{13,12},{... | collective-permute-start | bytes 393224 | tf_op jit(solution)/shard_map/ppermute | solution.py:25
  825.8 25.4 %collective-permute-start.9 = (f32[8,1,1,4096]{3,0,2,1:T(8,128)S(1)}, f32[8,1,1,4096]{3,0,2,1:T(8,128)S(1)}, u32[]{:S(2)}, u32[]{:S(2)}) collective-permute-start(f32[8,1,1,4096]{3,0,2,1:T(8,128)S(1)} %copy.346), channel_id=1, source_target_pairs={{0,1},{1,2},{2,3},{4,5},{5,6},{6,7},{8,9},{9,10},{10,11},{12,13},{... | collective-permute-start | bytes 393224 | tf_op jit(solution)/shard_map/ppermute | solution.py:22
  832.0 22.5 %collective-permute-start.2 = (f32[8,1,1,4096]{3,0,2,1:T(8,128)S(1)}, f32[8,1,1,4096]{3,0,2,1:T(8,128)S(1)}, u32[]{:S(2)}, u32[]{:S(2)}) collective-permute-start(f32[8,1,1,4096]{3,0,2,1:T(8,128)S(1)} %copy.327), channel_id=1, source_target_pairs={{1,0},{2,1},{3,2},{5,4},{6,5},{7,6},{9,8},{10,9},{11,10},{13,12},{... | collective-permute-start | bytes 393224 | tf_op jit(solution)/shard_map/ppermute | solution.py:25
  835.3 25.5 %collective-permute-start.3 = (f32[8,1,1,4096]{3,0,2,1:T(8,128)S(1)}, f32[8,1,1,4096]{3,0,2,1:T(8,128)S(1)}, u32[]{:S(2)}, u32[]{:S(2)}) collective-permute-start(f32[8,1,1,4096]{3,0,2,1:T(8,128)S(1)} %copy.329), channel_id=1, source_target_pairs={{0,1},{1,2},{2,3},{4,5},{5,6},{6,7},{8,9},{9,10},{10,11},{12,13},{... | collective-permute-start | bytes 393224 | tf_op jit(solution)/shard_map/ppermute | solution.py:22
  841.5 32.9 %collective-permute-start.14 = (f32[8,1,1,4096]{3,0,2,1:T(8,128)S(1)}, f32[8,1,1,4096]{3,0,2,1:T(8,128)S(1)}, u32[]{:S(2)}, u32[]{:S(2)}) collective-permute-start(f32[8,1,1,4096]{3,0,2,1:T(8,128)S(1)} %copy.361), channel_id=1, source_target_pairs={{1,0},{2,1},{3,2},{5,4},{6,5},{7,6},{9,8},{10,9},{11,10},{13,12},{... | collective-permute-start | bytes 393224 | tf_op jit(solution)/shard_map/ppermute | solution.py:25
  844.9 35.9 %collective-permute-start.15 = (f32[8,1,1,4096]{3,0,2,1:T(8,128)S(1)}, f32[8,1,1,4096]{3,0,2,1:T(8,128)S(1)}, u32[]{:S(2)}, u32[]{:S(2)}) collective-permute-start(f32[8,1,1,4096]{3,0,2,1:T(8,128)S(1)} %copy.363), channel_id=1, source_target_pairs={{0,1},{1,2},{2,3},{4,5},{5,6},{6,7},{8,9},{9,10},{10,11},{12,13},{... | collective-permute-start | bytes 393224 | tf_op jit(solution)/shard_map/ppermute | solution.py:22
  851.1 33.0 %collective-permute-start.20 = (f32[8,1,1,4096]{3,0,2,1:T(8,128)S(1)}, f32[8,1,1,4096]{3,0,2,1:T(8,128)S(1)}, u32[]{:S(2)}, u32[]{:S(2)}) collective-permute-start(f32[8,1,1,4096]{3,0,2,1:T(8,128)S(1)} %copy.378), channel_id=1, source_target_pairs={{1,0},{2,1},{3,2},{5,4},{6,5},{7,6},{9,8},{10,9},{11,10},{13,12},{... | collective-permute-start | bytes 393224 | tf_op jit(solution)/shard_map/ppermute | solution.py:25
  854.5 35.9 %collective-permute-start.21 = (f32[8,1,1,4096]{3,0,2,1:T(8,128)S(1)}, f32[8,1,1,4096]{3,0,2,1:T(8,128)S(1)}, u32[]{:S(2)}, u32[]{:S(2)}) collective-permute-start(f32[8,1,1,4096]{3,0,2,1:T(8,128)S(1)} %copy.380), channel_id=1, source_target_pairs={{0,1},{1,2},{2,3},{4,5},{5,6},{6,7},{8,9},{9,10},{10,11},{12,13},{... | collective-permute-start | bytes 393224 | tf_op jit(solution)/shard_map/ppermute | solution.py:22
  860.8 33.2 %collective-permute-start.10 = (f32[8,1,1,4096]{3,0,2,1:T(8,128)S(1)}, f32[8,1,1,4096]{3,0,2,1:T(8,128)S(1)}, u32[]{:S(2)}, u32[]{:S(2)}) collective-permute-start(f32[8,1,1,4096]{3,0,2,1:T(8,128)S(1)} %copy.349), channel_id=1, source_target_pairs={{1,0},{2,1},{3,2},{5,4},{6,5},{7,6},{9,8},{10,9},{11,10},{13,12},{... | collective-permute-start | bytes 393224 | tf_op jit(solution)/shard_map/ppermute | solution.py:25
  874.5 25.7 %collective-permute-start.11 = (f32[8,1,1,4096]{3,0,2,1:T(8,128)S(1)}, f32[8,1,1,4096]{3,0,2,1:T(8,128)S(1)}, u32[]{:S(2)}, u32[]{:S(2)}) collective-permute-start(f32[8,1,1,4096]{3,0,2,1:T(8,128)S(1)} %copy.351), channel_id=1, source_target_pairs={{0,1},{1,2},{2,3},{4,5},{5,6},{6,7},{8,9},{9,10},{10,11},{12,13},{... | collective-permute-start | bytes 393224 | tf_op jit(solution)/shard_map/ppermute | solution.py:22
  880.7 22.4 %collective-permute-start.4 = (f32[8,1,1,4096]{3,0,2,1:T(8,128)S(1)}, f32[8,1,1,4096]{3,0,2,1:T(8,128)S(1)}, u32[]{:S(2)}, u32[]{:S(2)}) collective-permute-start(f32[8,1,1,4096]{3,0,2,1:T(8,128)S(1)} %copy.332), channel_id=1, source_target_pairs={{1,0},{2,1},{3,2},{5,4},{6,5},{7,6},{9,8},{10,9},{11,10},{13,12},{... | collective-permute-start | bytes 393224 | tf_op jit(solution)/shard_map/ppermute | solution.py:25
  884.2 25.2 %collective-permute-start.5 = (f32[8,1,1,4096]{3,0,2,1:T(8,128)S(1)}, f32[8,1,1,4096]{3,0,2,1:T(8,128)S(1)}, u32[]{:S(2)}, u32[]{:S(2)}) collective-permute-start(f32[8,1,1,4096]{3,0,2,1:T(8,128)S(1)} %copy.334), channel_id=1, source_target_pairs={{0,1},{1,2},{2,3},{4,5},{5,6},{6,7},{8,9},{9,10},{10,11},{12,13},{... | collective-permute-start | bytes 393224 | tf_op jit(solution)/shard_map/ppermute | solution.py:22
  890.4 20.6 %collective-permute-start.16 = (f32[8,1,1,4096]{3,0,2,1:T(8,128)S(1)}, f32[8,1,1,4096]{3,0,2,1:T(8,128)S(1)}, u32[]{:S(2)}, u32[]{:S(2)}) collective-permute-start(f32[8,1,1,4096]{3,0,2,1:T(8,128)S(1)} %copy.366), channel_id=1, source_target_pairs={{1,0},{2,1},{3,2},{5,4},{6,5},{7,6},{9,8},{10,9},{11,10},{13,12},{... | collective-permute-start | bytes 393224 | tf_op jit(solution)/shard_map/ppermute | solution.py:25
  894.0 17.2 %collective-permute-start.17 = (f32[8,1,1,4096]{3,0,2,1:T(8,128)S(1)}, f32[8,1,1,4096]{3,0,2,1:T(8,128)S(1)}, u32[]{:S(2)}, u32[]{:S(2)}) collective-permute-start(f32[8,1,1,4096]{3,0,2,1:T(8,128)S(1)} %copy.368), channel_id=1, source_target_pairs={{0,1},{1,2},{2,3},{4,5},{5,6},{6,7},{8,9},{9,10},{10,11},{12,13},{... | collective-permute-start | bytes 393224 | tf_op jit(solution)/shard_map/ppermute | solution.py:22
  969.7 275.5 %all-to-all-start.1 = ((f32[128,1,256]{2,1,0:T(1,128)}), f32[128,1,256]{2,1,0:T(1,128)S(1)}, u32[]{:S(2)}, u32[]{:S(2)}) async-start(f32[128,1,256]{2,1,0:T(1,128)} %reshape.107), calls=%async_computation.1 | async-start | bytes 262144 | tf_op jit(solution)/shard_map/all_to_all | solution.py:79
  975.5 268.4 %all-reduce.26.cloned.1.call-start = ((), (), s32[]{:S(2)}) async-start(), calls=%async_computation.2 | async-start | bytes 131072 | tf_op jit(solution)/shard_map/psum | solution.py:81
  (5 other events, 1000.4 us)
Sparse Core Ops, SparseCore 0:
  981.3 262.5 all-reduce.25
where the time goes:
time: 1260 us; the launch traced here: 1250 us
  blocking collectives  768 us (61%)
  waiting for transfers between devices  268 us (21%)
  starting transfers between devices  106 us (8%)
  local copies, waits for them, and re-layouts  52.8 us (4%)
  other arithmetic  44.6 us (4%)
  between operations  15.4 us (1%)
    all_gather x4, blocking collectives, local(): gathered = lax.all_gather(orbital_block, 'pot', axis=2, tiled=True)  746 us
    psum x1, waiting for transfers between devices, local(): summed_all = lax.psum(partial_margins, ('pot', 'grid'))  268 us
    ppermute x12, starting transfers between devices, padded_2(): lax.ppermute(lax.slice_in_dim(block, block.shape[dim] - width, None, axis...  74.2 us
    all_gather x4, local copies, waits for them, and re-layouts, local(): gathered = lax.all_gather(orbital_block, 'pot', axis=2, tiled=True)  31.5 us
    ppermute x12, starting transfers between devices, padded_2(): lax.ppermute(lax.slice_in_dim(block, 0, width, axis=dim), axis, backward)  26 us
  transfers between devices with their start and end apart: 26, of which 1 were waited for; matrix products, arithmetic and copies ran while one was open for 2% of the time, Pallas kernels for 0%

commit v1 on v0

v1 whole, which is shorter than its diff:
```python
import functools

import jax
import jax.numpy as jnp
from jax import lax
from jax.experimental import pallas as pl
from jax.experimental.pallas import tpu as pltpu
from jax.sharding import PartitionSpec as P

MESH = pl.DeviceIdType.MESH
F32 = jnp.float32
BF16 = jnp.bfloat16
NZ = 32
NPAIR = 32
ROWS2D = [(dz, dy) for dz in range(-3, 4) for dy in range(-3, 4) if abs(dz) + abs(dy) <= 3]
INDEX2D = {pair: number for number, pair in enumerate(ROWS2D)}
OFFSETS = [
    (dz, dy, dx)
    for dz, dy in ROWS2D
    for dx in range(-3, 4)
    if abs(dz) + abs(dy) + abs(dx) <= 3
]
COUNT = len(OFFSETS)
LINES = sorted({(3 + zl + dz, 3 + yl + dy) for dz, dy in ROWS2D for zl in range(2) for yl in range(2)})
FAR = 1e30


def tile_of(p):
    core, x, y, low = p % 2, (p // 2) % 4, (p // 8) % 8, p // 64
    return low * 2 + core, y * 4 + x + (y % 2) * (3 - 2 * x)


def device_of(zp, yt):
    y, s = yt // 4, yt % 4
    return (zp // 2) * 64 + y * 8 + (s + (y % 2) * (3 - 2 * s)) * 2 + zp % 2


def place(zt, yt):
    return device_of(zt % 4, yt), zt // 4


def build_fields(zt, yt, loc, erow, orbs, pads, ls, bl, wf, pf):
    for m in range(5):
        pp = yt - 2 + m
        ok = jnp.logical_and(pp >= 0, pp < NPAIR)
        pc = jnp.clip(pp, 0, NPAIR - 1)
        column = loc[:, pl.ds(pl.multiple_of(pc * 128, 128), 128)]
        pads[m, 0:8, :] = jnp.full((8, 128), FAR, F32)
        pads[m, 40:48, :] = jnp.full((8, 128), FAR, F32)
        pads[m, 8:40, :] = jnp.where(ok, column, FAR)
        ls[m * 8 : m * 8 + 8, :] = pads[m, pl.ds(2 * zt + 5, 8), :]
    lt = ls[...].T
    for number, (k, r) in enumerate(LINES):
        m, yl = (r + 1) // 2, (r + 1) % 2
        c = m * 8 + k
        bl[number] = jnp.broadcast_to(lt[yl * 64 : yl * 64 + 64, c : c + 1], (64, 128))
    group = lax.broadcasted_iota(jnp.int32, (64, 128), 1) // 32
    group16 = lax.broadcasted_iota(jnp.int32, (16, 128), 1) // 32
    line_index = {line: number for number, line in enumerate(LINES)}
    shift3 = 3.0 - erow[...]
    zeros = jnp.zeros((8, 128), F32)
    for number, (dz, dy) in enumerate(ROWS2D):
        at = None
        lines = [(3 + zl + dz, 3 + yl + dy) for zl in range(2) for yl in range(2)]
        for l, line in enumerate(lines):
            here = bl[line_index[line]]
            at = here if at is None else jnp.where(group == l, here, at)
        w = jnp.where(at > 0.1 * FAR, 0.0, 0.4 / (at + shift3))
        wf[number, 0:8, :] = zeros
        wf[number, 72:80, :] = zeros
        wf[number, 8:72, :] = w
        pf[number, 0:8, :] = zeros
        pf[number, 72:80, :] = zeros
        for h in range(2):
            for xq in range(2):
                orb = None
                for l, (k, r) in enumerate(lines):
                    q, zl = (k + 1) // 2, (k + 1) % 2
                    unit = orbs[r, h, q].astype(F32)
                    shift = (l * 32 - zl * 64 - xq * 32) % 128
                    if shift:
                        unit = pltpu.roll(unit, shift, 1)
                    orb = unit if orb is None else jnp.where(group16 == l, unit, orb)
                x0 = h * 32 + xq * 16
                pf[number, 8 + x0 : 24 + x0, :] = orb * w[x0 : x0 + 16]


def build_products(wf, pf, sf, qb):
    def w(dz, dy, dx):
        return wf[INDEX2D[(dz, dy)], 8 + dx : 72 + dx, :]

    cross = [(0, 0), (1, 0), (-1, 0), (0, 1), (0, -1)]
    for number, (dz, dy) in enumerate(cross):
        i = INDEX2D[(dz, dy)]
        total = wf[i, 3:75, :] + wf[i, 5:77, :]
        for ez, ey in cross[1:]:
            total = total + wf[INDEX2D[(dz + ez, dy + ey)], 4:76, :]
        sf[number, 4:76, :] = total

    def s1(dz, dy, dx):
        return sf[cross.index((dz, dy)), 8 + dx : 72 + dx, :]

    def unit(axis, sign):
        return tuple(sign if a == axis else 0 for a in range(3))

    def plus(a, b):
        return tuple(x + y for x, y in zip(a, b))

    mine = -0.25 * pf[INDEX2D[(0, 0)], 8:72, :]
    for number, offset in enumerate(OFFSETS):
        dist = sum(abs(c) for c in offset)
        steps = []
        for axis in range(3):
            if offset[axis]:
                steps.append((unit(axis, 1 if offset[axis] > 0 else -1), abs(offset[axis])))
        if dist == 0:
            orb = 1.248 / w(0, 0, 0)
            path = orb + 1.6 * s1(0, 0, 0)
        elif dist == 1:
            e = offset
            w0, we = w(0, 0, 0), w(*e)
            path = 1.52 + w0 * (s1(0, 0, 0) - we) + we * s1(*e)
            for axis in range(3):
                if not e[axis]:
                    for sign in (1, -1):
                        b = unit(axis, sign)
                        path = path + w(*b) * w(*plus(b, e))
        elif dist == 2:
            if len(steps) == 1:
                path = 1.6 * w(*steps[0][0])
            else:
                path = 1.6 * (w(*steps[0][0]) + w(*steps[1][0]))
        elif len(steps) == 1:
            a = steps[0][0]
            path = w(*a) * w(*plus(a, a))
        elif len(steps) == 2:
            (a, b) = (steps[0][0], steps[1][0]) if steps[0][1] == 2 else (steps[1][0], steps[0][0])
            ab = w(*plus(a, b))
            path = w(*a) * (w(*plus(a, a)) + ab) + w(*b) * ab
        else:
            a, b, c = (s[0] for s in steps)
            ab, ac, bc = w(*plus(a, b)), w(*plus(a, c)), w(*plus(b, c))
            path = w(*a) * (ab + ac) + w(*b) * (ab + bc) + w(*c) * (ac + bc)
        dz, dy, dx = offset
        q = mine * pf[INDEX2D[(dz, dy)], 8 + dx : 72 + dx, :] * path
        high = q.astype(BF16)
        qb[number * 64 : number * 64 + 64, 0:128] = high
        qb[number * 64 : number * 64 + 64, 128:256] = (q - high.astype(F32)).astype(BF16)


def build_coefficients(qb, coef):
    k = lax.broadcasted_iota(jnp.int32, (256, 512), 0)
    n = lax.broadcasted_iota(jnp.int32, (256, 512), 1)
    spread = jnp.where((k % 128) // 32 == n // 128, 1.0, 0.0).astype(BF16)

    @pl.loop(0, 9)
    def _(step):
        rows = pl.ds(pl.multiple_of(step * 448, 448), 448)
        coef[rows, :] = jnp.dot(qb[rows, :], spread, preferred_element_type=F32)


def apply_stencil(own, halo, vf, coef):
    zeros = jnp.zeros((8, 128), F32)
    for number, (k, r) in enumerate(LINES):
        vf[number, 0:8, :] = zeros
        vf[number, 72:80, :] = zeros
        if 3 <= k <= 4 and 3 <= r <= 4:
            vf[number, 8:72, :] = own[k - 3, r - 3]
        else:
            vf[number, 8:72, :] = halo[k, r].astype(F32)
    line_index = {line: number for number, line in enumerate(LINES)}
    trial = []
    for l in range(4):
        zl, yl = l // 2, l % 2
        total = own[zl, yl]
        for number, (dz, dy, dx) in enumerate(OFFSETS):
            field = vf[line_index[(3 + zl + dz, 3 + yl + dy)], 8 + dx : 72 + dx, :]
            total = total + coef[number * 64 : number * 64 + 64, l * 128 : l * 128 + 128] * field
        trial.append(total)
    return trial


def finish(trial, factor, ug):
    columns = []
    for zl in range(2):
        plane = jnp.concatenate([trial[2 * zl], trial[2 * zl + 1]], axis=0)
        columns.append(plane.T.astype(BF16))
    gram = None
    for zl in range(2):
        ug[zl] = jnp.dot(factor[...], columns[zl], preferred_element_type=F32)
        part = lax.dot_general(columns[zl], columns[zl], (((1,), (1,)), ((), ())), preferred_element_type=F32)
        gram = part if gram is None else gram + part
    ug[2] = gram * (1.0 / 131072.0)


def local_kernel(coords, own, halo, orbs, loc, erow, factor, ug, pads, ls, bl, wf, pf, sf, qb, coef, vf):
    zt, yt = coords()
    build_fields(zt, yt, loc, erow, orbs, pads, ls, bl, wf, pf)
    build_products(wf, pf, sf, qb)
    build_coefficients(qb, coef)
    finish(apply_stencil(own, halo, vf, coef), factor, ug)


LOCAL_SCRATCH = [
    pltpu.VMEM((5, 48, 128), F32),
    pltpu.VMEM((128, 128), F32),
    pltpu.VMEM((len(LINES), 64, 128), F32),
    pltpu.VMEM((len(ROWS2D), 80, 128), F32),
    pltpu.VMEM((len(ROWS2D), 80, 128), F32),
    pltpu.VMEM((5, 80, 128), F32),
    pltpu.VMEM((COUNT * 64, 256), BF16),
    pltpu.VMEM((COUNT * 64, 512), F32),
    pltpu.VMEM((len(LINES), 80, 128), F32),
]


def local_part(coords, own, halo, orbs, loc, erow, factor):
    vmem = pl.BlockSpec(memory_space=pltpu.VMEM)
    return pl.pallas_call(
        functools.partial(local_kernel, coords),
        out_shape=jax.ShapeDtypeStruct((3, 128, 128), F32),
        in_specs=[vmem] * 6,
        out_specs=vmem,
        scratch_shapes=LOCAL_SCRATCH,
        compiler_params=pltpu.CompilerParams(vmem_limit_bytes=48 * 1024 * 1024),
    )(own, halo, orbs, loc, erow, factor)


NEIGHBOURS = [
    (1, 0, 0, 2, 0, 2), (-1, 0, 0, 2, 0, 2), (0, 1, 0, 2, 0, 2), (0, -1, 0, 2, 0, 2),
    (2, 0, 1, 1, 0, 2), (-2, 0, 0, 1, 0, 2), (0, 2, 0, 2, 1, 1), (0, -2, 0, 2, 0, 1),
    (1, 1, 1, 1, 0, 2), (1, -1, 1, 1, 0, 2), (-1, 1, 0, 1, 0, 2), (-1, -1, 0, 1, 0, 2),
    (1, 1, 0, 1, 1, 1), (1, -1, 0, 1, 0, 1), (-1, 1, 1, 1, 1, 1), (-1, -1, 1, 1, 0, 1),
]
PEERS = sorted({(a, b) for a, b, *_ in NEIGHBOURS})


def coords_here():
    zp, yt = tile_of(lax.axis_index("pot"))
    return lax.axis_index("grid") * 4 + zp, yt


def inward_kernel(rows_in, orb_in, own, halo, orbs, recv, lines, packed,
                  row_send, row_recv, slab_send, slab_recv, orb_send, orb_recv, halo_send, halo_recv):
    me, g = lax.axis_index("pot"), lax.axis_index("grid")
    zp, yt = tile_of(me)
    zt = g * 4 + zp
    up, down = (g + 1) % 4, (g + 3) % 4

    barrier = pltpu.get_barrier_semaphore()

    @pl.loop(1, 128)
    def _(step):
        pl.semaphore_signal(barrier, inc=1, device_id=((me + step) % 128, g), device_id_type=MESH)

    for other in (up, down):
        pl.semaphore_signal(barrier, inc=1, device_id=(me, other), device_id_type=MESH)
    for a, b in PEERS:
        peer = place((zt + a) % 16, (yt + b) % 32)
        pl.semaphore_signal(barrier, inc=1, device_id=peer, device_id_type=MESH)
    pl.semaphore_wait(barrier, 127 + 2 + len(PEERS))

    to_up = pltpu.make_async_remote_copy(
        orb_in.at[2:4], packed.at[0:2], slab_send.at[0], slab_recv.at[0], device_id=(me, up), device_id_type=MESH)
    to_down = pltpu.make_async_remote_copy(
        orb_in.at[0:2], packed.at[6:8], slab_send.at[1], slab_recv.at[1], device_id=(me, down), device_id_type=MESH)
    to_up.start()
    to_down.start()
    packed[2:6] = orb_in[...]

    @pl.loop(1, 128)
    def _(step):
        to = (me + step) % 128
        to_zp, to_yt = tile_of(to)
        pltpu.make_async_remote_copy(
            rows_in.at[:, to_zp * 32 + to_yt, :], recv.at[:, me, :], row_send, row_recv,
            device_id=(to, g), device_id_type=MESH).start()

    keep = pltpu.make_async_copy(rows_in.at[:, zp * 32 + yt, :], recv.at[:, me, :], row_recv)
    keep.start()
    to_up.wait()
    to_down.wait()

    row, half = me // 2, me % 2
    odd = row % 2
    for m in range(4):
        rr = 2 * m + 1 - odd
        to_yt = ((row + 3 - rr + 32 * 2) // 2) % 32
        for to_zp in range(4):
            to = device_of(to_zp, to_yt)
            source, target = packed.at[to_zp : to_zp + 5], orbs.at[rr, half]

            @pl.when(to != me)
            def _():
                pltpu.make_async_remote_copy(
                    source, target, orb_send, orb_recv, device_id=(to, g), device_id_type=MESH).start()

            @pl.when(to == me)
            def _():
                pltpu.make_async_copy(source, target, orb_recv).start()

    pltpu.make_async_copy(recv, recv, row_recv).wait()
    for zl in range(2):
        plane = recv[zl].T
        for yl in range(2):
            line = plane[yl * 64 : yl * 64 + 64]
            own[zl, yl] = line
            lines[zl, yl] = line.astype(BF16)
    copies = []
    for number, (a, b, z0, nz, y0, ny) in enumerate(NEIGHBOURS):
        peer = place((zt + a) % 16, (yt + b) % 32)
        zz, yy = 3 - 2 * a + z0, 3 - 2 * b + y0
        copies.append(pltpu.make_async_remote_copy(
            lines.at[z0 : z0 + nz, y0 : y0 + ny], halo.at[zz : zz + nz, yy : yy + ny],
            halo_send.at[number], halo_recv.at[number], device_id=peer, device_id_type=MESH))
        copies[-1].start()
    pltpu.make_async_copy(orbs, orbs, orb_recv).wait()
    for copy in copies:
        copy.wait()
    pltpu.make_async_copy(rows_in.at[:, 0:127, :], rows_in.at[:, 0:127, :], row_send).wait()

    count = 16
    same = 0
    for m in range(4):
        rr = 2 * m + 1 - odd
        to_yt = ((row + 3 - rr + 32 * 2) // 2) % 32
        for to_zp in range(4):
            same = same + jnp.where(device_of(to_zp, to_yt) == me, 1, 0)

    @pl.when(same == 0)
    def _():
        pltpu.make_async_copy(orbs, orbs, orb_send).wait()

    @pl.when(same != 0)
    def _():
        flat = orbs.at[0:7]
        pltpu.make_async_copy(flat, flat, orb_send).wait()
        pltpu.make_async_copy(orbs.at[7, 0], orbs.at[7, 0], orb_send).wait()


def inward(rows_in, orb_in):
    vmem = pl.BlockSpec(memory_space=pltpu.VMEM)
    return pl.pallas_call(
        inward_kernel,
        out_shape=(
            jax.ShapeDtypeStruct((2, 2, 64, 128), F32),
            jax.ShapeDtypeStruct((8, 8, 64, 128), BF16),
            jax.ShapeDtypeStruct((8, 2, 5, 16, 128), BF16),
        ),
        in_specs=[vmem] * 2,
        out_specs=(vmem,) * 3,
        scratch_shapes=[
            pltpu.VMEM((2, 128, 128), F32),
            pltpu.VMEM((2, 2, 64, 128), BF16),
            pltpu.VMEM((8, 16, 128), BF16),
            pltpu.SemaphoreType.DMA, pltpu.SemaphoreType.DMA,
            pltpu.SemaphoreType.DMA((2,)), pltpu.SemaphoreType.DMA((2,)),
            pltpu.SemaphoreType.DMA, pltpu.SemaphoreType.DMA,
            pltpu.SemaphoreType.DMA((16,)), pltpu.SemaphoreType.DMA((16,)),
        ],
        compiler_params=pltpu.CompilerParams(
            collective_id=0, has_side_effects=True, vmem_limit_bytes=32 * 1024 * 1024),
    )(rows_in, orb_in)


def outward_kernel(ug, out, margins, back, parts, send, recv, part_send, part_recv):
    me, g = lax.axis_index("pot"), lax.axis_index("grid")
    zp, yt = tile_of(me)
    slot = zp * 32 + yt
    barrier = pltpu.get_barrier_semaphore()

    @pl.loop(1, 128)
    def _(step):
        pl.semaphore_signal(barrier, inc=1, device_id=((me + step) % 128, g), device_id_type=MESH)

    for step in range(1, 4):
        pl.semaphore_signal(barrier, inc=1, device_id=(me, (g + step) % 4), device_id_type=MESH)
    pl.semaphore_wait(barrier, 130)

    @pl.loop(1, 128)
    def _(step):
        to = (me + step) % 128
        pltpu.make_async_remote_copy(
            ug.at[:, to, :], back.at[:, slot, :], send, recv, device_id=(to, g), device_id_type=MESH).start()

    pltpu.make_async_copy(ug.at[:, me, :], back.at[:, slot, :], recv).start()
    pltpu.make_async_copy(back, back, recv).wait()
    parts[0] = jnp.broadcast_to(jnp.sum(back[2], axis=0, keepdims=True), (8, 128))
    copies = []
    for step in range(1, 4):
        copies.append(pltpu.make_async_remote_copy(
            parts.at[0], parts.at[4 - step], part_send.at[step - 1], part_recv.at[step - 1],
            device_id=(me, (g + step) % 4), device_id_type=MESH))
        copies[-1].start()
    for z in range(8):
        rows = back[z % 2, (z // 2) * 32 : (z // 2) * 32 + 32, :]
        for y in range(32):
            out[0, z : z + 1, y * 128 : y * 128 + 128] = rows[y : y + 1]
    for copy in copies:
        copy.wait()
    total = None
    for slab in range(4):
        part = parts[(slab - g + 4) % 4]
        total = part if total is None else total + part
    margins[...] = total[0:1]
    pltpu.make_async_copy(ug.at[:, 0:127, :], ug.at[:, 0:127, :], send).wait()


def outward(ug):
    vmem = pl.BlockSpec(memory_space=pltpu.VMEM)
    return pl.pallas_call(
        outward_kernel,
        out_shape=(jax.ShapeDtypeStruct((1, 8, 4096), F32), jax.ShapeDtypeStruct((1, 128), F32)),
        in_specs=[vmem],
        out_specs=(vmem,) * 2,
        scratch_shapes=[
            pltpu.VMEM((3, 128, 128), F32),
            pltpu.VMEM((4, 8, 128), F32),
            pltpu.SemaphoreType.DMA, pltpu.SemaphoreType.DMA,
            pltpu.SemaphoreType.DMA((3,)), pltpu.SemaphoreType.DMA((3,)),
        ],
        compiler_params=pltpu.CompilerParams(
            collective_id=1, has_side_effects=True, vmem_limit_bytes=32 * 1024 * 1024),
    )(ug)


def prepared(potentials, orbitals, energies):
    rows = potentials.reshape(4, 2, 32, 128).transpose(1, 0, 2, 3).reshape(2, 128, 128)
    packed = orbitals.reshape(32, 4, 2, 2, 16).transpose(1, 4, 2, 3, 0).reshape(4, 16, 128)
    return rows, packed, jnp.tile(energies, 4).reshape(1, 128)


def local(potentials, orbitals, energies, local_potential, inverse_factor):
    rows, packed, erow = prepared(potentials, orbitals, energies)
    own, halo, orbs = inward(rows, packed)
    ug = local_part(coords_here, own, halo, orbs, local_potential, erow, inverse_factor)
    return outward(ug)


def solution(mesh):
    in_specs = (P("pot", "grid", None), P(None, "grid", "pot"), P(), P(), P())
    out_specs = (P("pot", "grid", None), P("pot", None))
    return jax.shard_map(local, mesh=mesh, in_specs=in_specs, out_specs=out_specs, check_vma=False)
```

time: 1260 us -> 83 us (0.07)
  blocking collectives: 768 us -> 0 us
  waiting for transfers between devices: 268 us -> 0 us
  starting transfers between devices: 106 us -> 0 us
  Pallas kernels: 0 us -> 77.9 us
  local copies, waits for them, and re-layouts: 52.8 us -> 4.03 us
  other arithmetic: 44.6 us -> 0 us
  between operations: 15.4 us -> 0.71 us
    all_gather x4 -> x0, blocking collectives: 746 us -> none  [local(): gathered = lax.all_gather(orbital_block, 'pot', axis=2, tiled=True)]
    psum x1 -> x0, waiting for transfers between devices: 268 us -> none  [local(): summed_all = lax.psum(partial_margins, ('pot', 'grid'))]
    ppermute x24 -> x0, starting transfers between devices: 100 us -> none  [the longest x12 74.2 us: padded_2(): lax.ppermute(lax.slice_in_dim(block, block.shape[dim] - width, None, axis...]
    pallas_call x0 -> x3, Pallas kernels: none -> 77.9 us  [the longest x1 39 us: outward(): pl.pallas_call(outward_kernel, out_shape=(jax.ShapeDtypeStruct((1, 8, 409...]
    all_gather x4 -> x0, local copies, waits for them, and re-layouts: 31.5 us -> none  [local(): gathered = lax.all_gather(orbital_block, 'pot', axis=2, tiled=True)]
    unnamed x1 -> x0, other arithmetic: 22.4 us -> none
    all_to_all x1 -> x0, blocking collectives: 21.8 us -> none  [local(): lax.all_to_all(trial_block, 'pot', split_axis=2, concat_axis=0, tiled=True)]
    add x9 -> x0, other arithmetic: 13.1 us -> none  [the longest x8 12.2 us: absorb(): answer + DAMPING * (source - diagonal * answer + 0.5 * nearby) / diagonal]
  transfers between devices with their start and end apart: 26 -> 0, of which waited for: 1 -> 0; matrix products, arithmetic and copies ran while one was open for 2% -> 0% of each run, Pallas kernels for 0% -> 0%
where the time goes in v1:
time: 83 us; the launch traced here: 82.7 us
  Pallas kernels  77.9 us (94%)
  local copies, waits for them, and re-layouts  4.03 us (5%)
    pallas_call x1, Pallas kernels, outward(): pl.pallas_call(outward_kernel, out_shape=(jax.ShapeDtypeStruct((1, 8, 409...  39 us
    pallas_call x1, Pallas kernels, inward(): pl.pallas_call(inward_kernel, out_shape=(jax.ShapeDtypeStruct((2, 2, 64,...  33.3 us
    pallas_call x1, Pallas kernels, local_part(): pl.pallas_call(functools.partial(local_kernel, coords), out_shape=jax.Sha...  5.64 us
    unnamed x8, local copies, waits for them, and re-layouts  3.07 us

profile of v1, /device:TPU:1, one launch (start us, length us, event | category | flops | bytes accessed | tf_op | source)
XLA Modules:
  0.0 82.7 jit_solution(6441726647363070914)
XLA Ops:
  0.6 0.0 copy-start
  0.6 0.7 tile.2
  1.4 0.1 reshape_tile.3.erow
  1.4 1.0 %copy.10 = bf16[32,8,32]{0,2,1:T(8,128)(2,1)S(1)} copy(bf16[32,8,32]{2,1,0:T(8,128)(2,1)} %param.6) | data formatting | bytes 32768 | tf_op args[1]
  2.4 0.1 copy.11
  2.5 0.1 reshape.20.orb_in
  2.6 0.9 %copy.12 = f32[1,8,32,128]{3,2,1,0:T(8,128)S(1)} copy(f32[1,8,32,128]{3,1,2,0:T(8,128)} %bitcast.13) | data formatting | bytes 262144
  3.5 0.0 copy-start.1
  3.5 33.3 %shard_map.68 = (f32[2,2,64,128]{3,2,1,0:T(8,128)S(1)}, bf16[8,8,64,128]{3,2,1,0:T(8,128)(2,1)S(1)}, bf16[8,2,5,16,128]{4,3,2,1,0:T(8,128)(2,1)S(1)}) custom-call(f32[2,128,128]{2,1,0:T(8,128)S(1)} %bitcast.10, bf16[4,16,128]{2,1,0:T(8,128)(2,1)S(1)} %reshape.20.orb_in), custom_call_target="tpu_custom_call" | custom-call | tf_op jit(solution)/shard_map/pallas_call | solution.py:343
  36.9 0.0 copy-done
  36.9 0.0 copy-done.1
  36.9 5.6 %shard_map.69.ug = f32[3,128,128]{2,1,0:T(8,128)S(1)} custom-call(f32[2,2,64,128]{3,2,1,0:T(8,128)S(1)} %get-tuple-element.5.own, bf16[8,8,64,128]{3,2,1,0:T(8,128)(2,1)S(1)} %get-tuple-element.6.halo, bf16[8,2,5,16,128]{4,3,2,1,0:T(8,128)(2,1)S(1)} %get-tuple-element.7.orbs, f32[32,4096]{1,0:T(8,128)S(1)} %copy-done, f32[1,128]{1,0:T(1,128)S(1)} %reshape_tile.3.erow, ...), custom_call_target="tpu_custom_call" | custom-call | tf_op jit(solution)/shard_map/pallas_call | solution.py:219
  42.5 39.0 %shard_map.70 = (f32[1,8,4096]{2,1,0:T(8,128)S(1)}, f32[1,128]{1,0:T(1,128)S(1)}) custom-call(f32[3,128,128]{2,1,0:T(8,128)S(1)} %shard_map.69.ug), custom_call_target="tpu_custom_call" | custom-call | tf_op jit(solution)/shard_map/pallas_call | solution.py:411
  81.5 0.7 copy.15
  82.2 0.5 copy.16
  (1 shorter events, 0.0 us)
Async XLA Ops:
  0.6 36.2 %copy-start = (f32[32,4096]{1,0:T(8,128)S(1)}, f32[32,4096]{1,0:T(8,128)}, u32[]{:S(2)}) copy-start(f32[32,4096]{1,0:T(8,128)} %loc.1) | copy-start | bytes 1572868
  3.5 33.4 %copy-start.1 = (bf16[128,128]{1,0:T(8,128)(2,1)S(1)}, bf16[128,128]{1,0:T(8,128)(2,1)}, u32[]{:S(2)}) copy-start(bf16[128,128]{1,0:T(8,128)(2,1)} %factor.1) | copy-start | bytes 98308

commit v2 on v1

v2 whole, which is shorter than its diff:
```python
import jax
import jax.numpy as jnp
from jax import lax
from jax.experimental import pallas as pl
from jax.experimental.pallas import tpu as pltpu
from jax.sharding import PartitionSpec as P

MESH = pl.DeviceIdType.MESH
F32 = jnp.float32
BF16 = jnp.bfloat16
NZ = 32
NPAIR = 32
ROWS2D = [(dz, dy) for dz in range(-3, 4) for dy in range(-3, 4) if abs(dz) + abs(dy) <= 3]
INDEX2D = {pair: number for number, pair in enumerate(ROWS2D)}
OFFSETS = [
    (dz, dy, dx)
    for dz, dy in ROWS2D
    for dx in range(-3, 4)
    if abs(dz) + abs(dy) + abs(dx) <= 3
]
COUNT = len(OFFSETS)
LINES = sorted({(3 + zl + dz, 3 + yl + dy) for dz, dy in ROWS2D for zl in range(2) for yl in range(2)})
LINE_INDEX = {line: number for number, line in enumerate(LINES)}
CROSS = [(0, 0), (1, 0), (-1, 0), (0, 1), (0, -1)]
FAR = 1e30


def tile_of(p):
    core, x, y, low = p % 2, (p // 2) % 4, (p // 8) % 8, p // 64
    return low * 2 + core, y * 4 + x + (y % 2) * (3 - 2 * x)


def device_of(zp, yt):
    y, s = yt // 4, yt % 4
    return (zp // 2) * 64 + y * 8 + (s + (y % 2) * (3 - 2 * s)) * 2 + zp % 2


def place(zt, yt):
    return device_of(zt % 4, yt), zt // 4


def line_sets(dz, dy):
    return [(3 + zl + dz, 3 + yl + dy) for zl in range(2) for yl in range(2)]


def build_weights(zt, yt, loc, energies, pads, ls, bl, wf, sf):
    for m in range(5):
        pp = yt - 2 + m
        ok = jnp.logical_and(pp >= 0, pp < NPAIR)
        pc = jnp.clip(pp, 0, NPAIR - 1)
        column = loc[:, pl.ds(pl.multiple_of(pc * 128, 128), 128)]
        pads[m, 0:8, :] = jnp.full((8, 128), FAR, F32)
        pads[m, 40:48, :] = jnp.full((8, 128), FAR, F32)
        pads[m, 8:40, :] = jnp.where(ok, column, FAR)
        ls[m * 8 : m * 8 + 8, :] = pads[m, pl.ds(2 * zt + 5, 8), :]
    lt = ls[...].T
    for number, (k, r) in enumerate(LINES):
        m, yl = (r + 1) // 2, (r + 1) % 2
        c = m * 8 + k
        bl[number] = jnp.broadcast_to(lt[yl * 64 : yl * 64 + 64, c : c + 1], (64, 128))
    group = lax.broadcasted_iota(jnp.int32, (64, 128), 1) // 32
    row = energies[...]
    shift3 = 3.0 - jnp.concatenate([row, row, row, row], axis=1)
    zeros = jnp.zeros((8, 128), F32)
    for number, (dz, dy) in enumerate(ROWS2D):
        at = None
        for l, line in enumerate(line_sets(dz, dy)):
            here = bl[LINE_INDEX[line]]
            at = here if at is None else jnp.where(group == l, here, at)
        wf[number, 0:8, :] = zeros
        wf[number, 72:80, :] = zeros
        wf[number, 8:72, :] = jnp.where(at > 0.1 * FAR, 0.0, 0.4 / (at + shift3))
    for number, (dz, dy) in enumerate(CROSS):
        i = INDEX2D[(dz, dy)]
        total = wf[i, 3:75, :] + wf[i, 5:77, :]
        for ez, ey in CROSS[1:]:
            total = total + wf[INDEX2D[(dz + ez, dy + ey)], 4:76, :]
        sf[number, 4:76, :] = total


def build_orbitals(orbs, wf, pf):
    group = lax.broadcasted_iota(jnp.int32, (16, 128), 1) // 32
    zeros = jnp.zeros((8, 128), F32)
    for number, (dz, dy) in enumerate(ROWS2D):
        pf[number, 0:8, :] = zeros
        pf[number, 72:80, :] = zeros
        for h in range(2):
            for xq in range(2):
                orb = None
                for l, (k, r) in enumerate(line_sets(dz, dy)):
                    q, zl = (k + 1) // 2, (k + 1) % 2
                    unit = orbs[q, r, h].astype(F32)
                    shift = (l * 32 - zl * 64 - xq * 32) % 128
                    if shift:
                        unit = pltpu.roll(unit, shift, 1)
                    orb = unit if orb is None else jnp.where(group == l, unit, orb)
                x0 = 8 + h * 32 + xq * 16
                pf[number, x0 : x0 + 16, :] = orb * wf[number, x0 : x0 + 16, :]


def build_products(wf, pf, sf, qb):
    def w(dz, dy, dx):
        return wf[INDEX2D[(dz, dy)], 8 + dx : 72 + dx, :]

    def s1(dz, dy, dx):
        return sf[CROSS.index((dz, dy)), 8 + dx : 72 + dx, :]

    def unit(axis, sign):
        return tuple(sign if a == axis else 0 for a in range(3))

    def plus(a, b):
        return tuple(x + y for x, y in zip(a, b))

    mine = -0.25 * pf[INDEX2D[(0, 0)], 8:72, :]
    for number, offset in enumerate(OFFSETS):
        dist = sum(abs(c) for c in offset)
        steps = []
        for axis in range(3):
            if offset[axis]:
                steps.append((unit(axis, 1 if offset[axis] > 0 else -1), abs(offset[axis])))
        if dist == 0:
            orb = 1.248 / w(0, 0, 0)
            path = orb + 1.6 * s1(0, 0, 0)
        elif dist == 1:
            e = offset
            w0, we = w(0, 0, 0), w(*e)
            path = 1.52 + w0 * (s1(0, 0, 0) - we) + we * s1(*e)
            for axis in range(3):
                if not e[axis]:
                    for sign in (1, -1):
                        b = unit(axis, sign)
                        path = path + w(*b) * w(*plus(b, e))
        elif dist == 2:
            if len(steps) == 1:
                path = 1.6 * w(*steps[0][0])
            else:
                path = 1.6 * (w(*steps[0][0]) + w(*steps[1][0]))
        elif len(steps) == 1:
            a = steps[0][0]
            path = w(*a) * w(*plus(a, a))
        elif len(steps) == 2:
            (a, b) = (steps[0][0], steps[1][0]) if steps[0][1] == 2 else (steps[1][0], steps[0][0])
            ab = w(*plus(a, b))
            path = w(*a) * (w(*plus(a, a)) + ab) + w(*b) * ab
        else:
            a, b, c = (s[0] for s in steps)
            ab, ac, bc = w(*plus(a, b)), w(*plus(a, c)), w(*plus(b, c))
            path = w(*a) * (ab + ac) + w(*b) * (ab + bc) + w(*c) * (ac + bc)
        dz, dy, dx = offset
        q = mine * pf[INDEX2D[(dz, dy)], 8 + dx : 72 + dx, :] * path
        high = q.astype(BF16)
        qb[number * 64 : number * 64 + 64, 0:128] = high
        qb[number * 64 : number * 64 + 64, 128:256] = (q - high.astype(F32)).astype(BF16)


def build_coefficients(qb, coef):
    k = lax.broadcasted_iota(jnp.int32, (256, 512), 0)
    n = lax.broadcasted_iota(jnp.int32, (256, 512), 1)
    spread = jnp.where((k % 128) // 32 == n // 128, 1.0, 0.0).astype(BF16)

    @pl.loop(0, 9)
    def _(step):
        rows = pl.ds(pl.multiple_of(step * 448, 448), 448)
        coef[rows, :] = jnp.dot(qb[rows, :], spread, preferred_element_type=F32)


def place_lines(source, inside, vf):
    zeros = jnp.zeros((8, 128), F32)
    for number, (k, r) in enumerate(LINES):
        here = 3 <= k <= 4 and 3 <= r <= 4
        if here != inside:
            continue
        vf[number, 0:8, :] = zeros
        vf[number, 72:80, :] = zeros
        vf[number, 8:72, :] = source[k - 3, r - 3] if here else source[k, r].astype(F32)


def apply_stencil(vf, coef):
    trial = []
    for l in range(4):
        zl, yl = l // 2, l % 2
        total = vf[LINE_INDEX[(3 + zl, 3 + yl)], 8:72, :]
        for number, (dz, dy, dx) in enumerate(OFFSETS):
            field = vf[LINE_INDEX[(3 + zl + dz, 3 + yl + dy)], 8 + dx : 72 + dx, :]
            total = total + coef[number * 64 : number * 64 + 64, l * 128 : l * 128 + 128] * field
        trial.append(total)
    return trial


def finish(trial, factor, ug):
    columns = []
    for zl in range(2):
        plane = jnp.concatenate([trial[2 * zl], trial[2 * zl + 1]], axis=0)
        columns.append(plane.T.astype(BF16))
    gram = None
    for zl in range(2):
        ug[zl] = jnp.dot(factor[...], columns[zl], preferred_element_type=F32)
        part = lax.dot_general(columns[zl], columns[zl], (((1,), (1,)), ((), ())), preferred_element_type=F32)
        gram = part if gram is None else gram + part
    ug[2] = gram * (1.0 / 131072.0)


NEIGHBOURS = [
    (1, 0, 0, 2, 0, 2), (-1, 0, 0, 2, 0, 2), (0, 1, 0, 2, 0, 2), (0, -1, 0, 2, 0, 2),
    (2, 0, 1, 1, 0, 2), (-2, 0, 0, 1, 0, 2), (0, 2, 0, 2, 1, 1), (0, -2, 0, 2, 0, 1),
    (1, 1, 1, 1, 0, 2), (1, -1, 1, 1, 0, 2), (-1, 1, 0, 1, 0, 2), (-1, -1, 0, 1, 0, 2),
    (1, 1, 0, 1, 1, 1), (1, -1, 0, 1, 0, 1), (-1, 1, 1, 1, 1, 1), (-1, -1, 1, 1, 0, 1),
]
ORB_NEIGHBOURS = [
    (1, 0, 0, 2), (-1, 0, 0, 2), (0, 1, 0, 2), (0, -1, 0, 2), (2, 0, 0, 2), (-2, 0, 0, 2),
    (1, 1, 0, 2), (1, -1, 0, 2), (-1, 1, 0, 2), (-1, -1, 0, 2), (0, 2, 1, 1), (0, -2, 0, 1),
]


def ring(distance, size):
    return min(distance, size - distance)


OTHERS = sorted(
    ((y, x, z, c) for y in range(8) for x in range(4) for z in range(2) for c in range(2) if y or x or z or c),
    key=lambda d: (-(ring(d[0], 8) + ring(d[1], 4) + d[2]), d),
)


def kernel(pot, orb_in, energies, loc, factor, out, margins,
           rows_in, recv, lines, own, halo, orbs, ug, back, parts, pads, ls, bl, wf, pf, sf, qb, coef, vf,
           row_send, row_recv, move_send, move_recv, orb_send, orb_recv, halo_send, halo_recv,
           back_send, back_recv, part_send, part_recv):
    me, g = lax.axis_index("pot"), lax.axis_index("grid")
    zp, yt = tile_of(me)
    zt = g * 4 + zp
    ys = [(me // 8 + d) % 8 * 8 for d in range(8)]
    xs = [(me // 2 + d) % 4 * 2 for d in range(4)]
    zs = [me // 64 * 64, (1 - me // 64) * 64]
    cs = [me % 2, 1 - me % 2]

    def others():
        for y, x, z, c in OTHERS:
            yield ys[y] + xs[x] + zs[z] + cs[c]

    def near(a, b):
        return place((zt + a + 16) % 16, (yt + b + 32) % 32)

    barrier = pltpu.get_barrier_semaphore()
    for to in others():
        pl.semaphore_signal(barrier, inc=1, device_id=(to, g), device_id_type=MESH)
    for step in range(1, 4):
        pl.semaphore_signal(barrier, inc=1, device_id=(me, (g + step) % 4), device_id_type=MESH)
    for a, b, *_ in ORB_NEIGHBOURS:
        pl.semaphore_signal(barrier, inc=1, device_id=near(a, b), device_id_type=MESH)

    for z in range(8):
        for y in range(32):
            to = device_of(z // 2, y)
            rows_in[z % 2, to : to + 1, :] = pot[0, z : z + 1, y * 128 : y * 128 + 128]
    build_weights(zt, yt, loc, energies, pads, ls, bl, wf, sf)
    pl.semaphore_wait(barrier, len(OTHERS) + 3 + len(ORB_NEIGHBOURS))

    row, half = me // 2, me % 2
    low, landing = row % 2, (row % 2) * 2 + half
    moves = []
    for to_zp in range(4):
        to = device_of(to_zp, row // 2)
        target = orbs.at[2, 3 + low, half]
        move = pltpu.make_async_remote_copy(
            orb_in.at[to_zp], target, move_send.at[to_zp], move_recv.at[landing],
            device_id=(to, g), device_id_type=MESH)
        moves.append((to, move))
        pl.when(to != me)(move.start)
        pl.when(to == me)(pltpu.make_async_copy(orb_in.at[to_zp], target, move_recv.at[landing]).start)

    for to in others():
        pltpu.make_async_remote_copy(
            rows_in.at[:, to, :], recv.at[:, me, :], row_send, row_recv,
            device_id=(to, g), device_id_type=MESH).start()
    pltpu.make_async_copy(rows_in.at[:, me, :], recv.at[:, me, :], row_recv).start()

    for yl in range(2):
        for h in range(2):
            landed = orbs.at[2, 3 + yl, h]
            pltpu.make_async_copy(landed, landed, move_recv.at[yl * 2 + h]).wait()
    orb_copies = []
    for number, (a, b, y0, ny) in enumerate(ORB_NEIGHBOURS):
        yy = 3 - 2 * b + y0
        orb_copies.append(pltpu.make_async_remote_copy(
            orbs.at[2, 3 + y0 : 3 + y0 + ny], orbs.at[2 - a, yy : yy + ny],
            orb_send.at[number], orb_recv.at[number], device_id=near(a, b), device_id_type=MESH))
        orb_copies[-1].start()

    pltpu.make_async_copy(recv, recv, row_recv).wait()
    for zl in range(2):
        plane = recv[zl].T
        for yl in range(2):
            line = plane[yl * 64 : yl * 64 + 64]
            own[zl, yl] = line
            lines[zl, yl] = line.astype(BF16)
    copies = []
    for number, (a, b, z0, nz, y0, ny) in enumerate(NEIGHBOURS):
        zz, yy = 3 - 2 * a + z0, 3 - 2 * b + y0
        copies.append(pltpu.make_async_remote_copy(
            lines.at[z0 : z0 + nz, y0 : y0 + ny], halo.at[zz : zz + nz, yy : yy + ny],
            halo_send.at[number], halo_recv.at[number], device_id=near(a, b), device_id_type=MESH))
        copies[-1].start()

    for copy in orb_copies:
        copy.wait_recv()
    build_orbitals(orbs, wf, pf)
    build_products(wf, pf, sf, qb)
    build_coefficients(qb, coef)
    place_lines(own, True, vf)
    for copy in copies:
        copy.wait_recv()
    place_lines(halo, False, vf)
    finish(apply_stencil(vf, coef), factor, ug)

    for to in others():
        pltpu.make_async_remote_copy(
            ug.at[:, to, :], back.at[:, me, :], back_send, back_recv,
            device_id=(to, g), device_id_type=MESH).start()
    pltpu.make_async_copy(ug.at[:, me, :], back.at[:, me, :], back_recv).start()
    for copy in orb_copies + copies:
        copy.wait_send()
    for to, move in moves:
        pl.when(to != me)(move.wait_send)
    pltpu.make_async_copy(rows_in.at[:, 0:127, :], rows_in.at[:, 0:127, :], row_send).wait()

    pltpu.make_async_copy(back, back, back_recv).wait()
    parts[0] = jnp.broadcast_to(jnp.sum(back[2], axis=0, keepdims=True), (8, 128))
    part_copies = []
    for step in range(1, 4):
        part_copies.append(pltpu.make_async_remote_copy(
            parts.at[0], parts.at[4 - step], part_send.at[step - 1], part_recv.at[step - 1],
            device_id=(me, (g + step) % 4), device_id_type=MESH))
        part_copies[-1].start()
    for z in range(8):
        for y in range(32):
            source = device_of(z // 2, y)
            out[0, z : z + 1, y * 128 : y * 128 + 128] = back[z % 2, source : source + 1, :]
    for copy in part_copies:
        copy.wait()
    total = None
    for slab in range(4):
        part = parts[(slab - g + 4) % 4]
        total = part if total is None else total + part
    margins[...] = total[0:1]
    pltpu.make_async_copy(ug.at[:, 0:127, :], ug.at[:, 0:127, :], back_send).wait()


def local(potentials, orbitals, energies, local_potential, inverse_factor):
    packed = orbitals.reshape(32, 4, 2, 2, 16).transpose(1, 4, 2, 3, 0).reshape(4, 16, 128)
    vmem = pl.BlockSpec(memory_space=pltpu.VMEM)
    dma = pltpu.SemaphoreType.DMA
    return pl.pallas_call(
        kernel,
        out_shape=(jax.ShapeDtypeStruct((1, 8, 4096), F32), jax.ShapeDtypeStruct((1, 128), F32)),
        in_specs=[vmem] * 5,
        out_specs=(vmem,) * 2,
        scratch_shapes=[
            pltpu.VMEM((2, 128, 128), F32),
            pltpu.VMEM((2, 128, 128), F32),
            pltpu.VMEM((2, 2, 64, 128), BF16),
            pltpu.VMEM((2, 2, 64, 128), F32),
            pltpu.VMEM((8, 8, 64, 128), BF16),
            pltpu.VMEM((5, 8, 2, 16, 128), BF16),
            pltpu.VMEM((3, 128, 128), F32),
            pltpu.VMEM((3, 128, 128), F32),
            pltpu.VMEM((4, 8, 128), F32),
            pltpu.VMEM((5, 48, 128), F32),
            pltpu.VMEM((128, 128), F32),
            pltpu.VMEM((len(LINES), 64, 128), F32),
            pltpu.VMEM((len(ROWS2D), 80, 128), F32),
            pltpu.VMEM((len(ROWS2D), 80, 128), F32),
            pltpu.VMEM((5, 80, 128), F32),
            pltpu.VMEM((COUNT * 64, 256), BF16),
            pltpu.VMEM((COUNT * 64, 512), F32),
            pltpu.VMEM((len(LINES), 80, 128), F32),
            dma, dma, dma((4,)), dma((4,)), dma((12,)), dma((12,)), dma((16,)), dma((16,)),
            dma, dma, dma((3,)), dma((3,)),
        ],
        compiler_params=pltpu.CompilerParams(
            collective_id=0, has_side_effects=True, vmem_limit_bytes=48 * 1024 * 1024),
    )(potentials, packed, energies.reshape(1, 32), local_potential, inverse_factor)


def solution(mesh):
    in_specs = (P("pot", "grid", None), P(None, "grid", "pot"), P(), P(), P())
    out_specs = (P("pot", "grid", None), P("pot", None))
    return jax.shard_map(local, mesh=mesh, in_specs=in_specs, out_specs=out_specs, check_vma=False)
```

time: 83 us -> 49.4 us (0.60)
  Pallas kernels: 77.9 us -> 44.5 us
    pallas_call x3 -> x1, Pallas kernels: 77.9 us -> 44.5 us  [local(): pl.pallas_call(kernel, out_shape=(jax.ShapeDtypeStruct((1, 8, 4096), F32)...]
    unnamed x8 -> x11, local copies, waits for them, and re-layouts: 3.07 us -> 3.88 us
where the time goes in v2:
time: 49.4 us; the launch traced here: 49.2 us
  Pallas kernels  44.5 us (90%)
  local copies, waits for them, and re-layouts  4.04 us (8%)
  between operations  0.68 us (1%)
    pallas_call x1, Pallas kernels, local(): pl.pallas_call(kernel, out_shape=(jax.ShapeDtypeStruct((1, 8, 4096), F32)...  44.5 us
    unnamed x11, local copies, waits for them, and re-layouts  3.88 us

profile of v2, /device:TPU:1, one launch (start us, length us, event | category | flops | bytes accessed | tf_op | source)
XLA Modules:
  0.0 49.2 jit_solution(1714274440036791568)
XLA Ops:
  0.6 1.0 %copy.8 = bf16[32,8,32]{0,2,1:T(8,128)(2,1)S(1)} copy(bf16[32,8,32]{2,1,0:T(8,128)(2,1)} %param.6) | data formatting | bytes 32768 | tf_op args[1]
  1.6 0.0 copy-start.1
  1.6 0.1 copy.9
  1.7 0.0 copy-start.2
  1.7 0.0 copy-start.3
  1.7 0.1 reshape.14.orb_in
  1.8 0.7 %copy-done.1 = f32[1,8,4096]{2,1,0:T(8,128)S(1)} copy-done((f32[1,8,4096]{2,1,0:T(8,128)S(1)}, f32[1,8,4096]{2,1,0:T(8,128)}, u32[]{:S(2)}) %copy-start.1) | copy-done | bytes 131096
  2.5 0.0 copy-done.2
  2.5 0.0 copy-done.3
  2.5 0.0 copy-start
  2.5 1.0 %copy-done = f32[32,4096]{1,0:T(8,128)S(1)} copy-done((f32[32,4096]{1,0:T(8,128)S(1)}, f32[32,4096]{1,0:T(8,128)}, u32[]{:S(2)}) %copy-start) | copy-done | bytes 524312
  3.5 44.5 %shard_map.68 = (f32[1,8,4096]{2,1,0:T(8,128)S(1)}, f32[1,128]{1,0:T(1,128)S(1)}) custom-call(f32[1,8,4096]{2,1,0:T(8,128)S(1)} %copy-done.1, bf16[4,16,128]{2,1,0:T(8,128)(2,1)S(1)} %reshape.14.orb_in, f32[1,32]{1,0:T(1,128)S(1)} %bitcast.4, f32[32,4096]{1,0:T(8,128)S(1)} %copy-done, bf16[128,128]{1,0:T(8,128)(2,1)S(1)} %copy-done.2), custom_call_target="tpu_custom_call" | custom-call | tf_op jit(solution)/shard_map/pallas_call | solution.py:353
  48.0 0.7 %copy.12 = f32[1,8,4096]{2,1,0:T(8,128)} copy(f32[1,8,4096]{2,1,0:T(8,128)S(1)} %get-tuple-element.4) | data formatting | bytes 262144
  48.7 0.5 %copy.13 = f32[1,128]{1,0:T(1,128)} copy(f32[1,128]{1,0:T(1,128)S(1)} %get-tuple-element.5) | data formatting | bytes 1024
Async XLA Ops:
  1.6 0.9 %copy-start.1 = (f32[1,8,4096]{2,1,0:T(8,128)S(1)}, f32[1,8,4096]{2,1,0:T(8,128)}, u32[]{:S(2)}) copy-start(f32[1,8,4096]{2,1,0:T(8,128)} %pot.1) | copy-start | bytes 393220
  1.7 0.8 %copy-start.2 = (bf16[128,128]{1,0:T(8,128)(2,1)S(1)}, bf16[128,128]{1,0:T(8,128)(2,1)}, u32[]{:S(2)}) copy-start(bf16[128,128]{1,0:T(8,128)(2,1)} %factor.1) | copy-start | bytes 98308
  1.7 0.8 %copy-start.3 = (f32[32]{0:T(128)S(1)}, f32[32]{0:T(128)}, u32[]{:S(2)}) copy-start(f32[32]{0:T(128)} %param.7) | copy-start | bytes 388
  2.5 1.0 %copy-start = (f32[32,4096]{1,0:T(8,128)S(1)}, f32[32,4096]{1,0:T(8,128)}, u32[]{:S(2)}) copy-start(f32[32,4096]{1,0:T(8,128)} %loc.1) | copy-start | bytes 1572868

commit v3 on v2

--- a/solution.py
+++ b/solution.py
@@ -43,15 +43,33 @@
     return [(3 + zl + dz, 3 + yl + dy) for zl in range(2) for yl in range(2)]
 
 
-def build_weights(zt, yt, loc, energies, pads, ls, bl, wf, sf):
+def pack_helpers():
+    n = lax.broadcasted_iota(jnp.int32, (512, 256), 0)
+    k = lax.broadcasted_iota(jnp.int32, (512, 256), 1)
+    want = (n % 32) * 8 + (n // 128) * 2 + (n // 32) % 2
+    choose = jnp.where(k == want, 1.0, 0.0).astype(BF16)
+    fold = lax.broadcasted_iota(jnp.int32, (16, 32), 1) % 16 == lax.broadcasted_iota(jnp.int32, (16, 32), 0)
+    return choose, jnp.where(fold, 1.0, 0.0).astype(BF16)
+
+
+def pack_orbitals(orb, choose, fold, packed):
+    flat = orb[...].astype(F32).reshape(256, 32).astype(BF16)
+    lanes = jnp.dot(choose, flat, preferred_element_type=F32)
+    row = lax.broadcasted_iota(jnp.int32, (512, 32), 0)
+    cell = lax.broadcasted_iota(jnp.int32, (512, 32), 1)
+    lanes = jnp.where(cell // 16 == (row // 64) % 2, lanes, 0.0).astype(BF16)
+    folded = lax.dot_general(fold, lanes, (((1,), (1,)), ((), ())), preferred_element_type=F32)
+    for pair in range(4):
+        packed[pair] = folded[:, pair * 128 : pair * 128 + 128].astype(BF16)
+
+
+def build_weights(zt, yt, columns, energies, pads, ls, bl, wf, sf):
     for m in range(5):
         pp = yt - 2 + m
         ok = jnp.logical_and(pp >= 0, pp < NPAIR)
-        pc = jnp.clip(pp, 0, NPAIR - 1)
-        column = loc[:, pl.ds(pl.multiple_of(pc * 128, 128), 128)]
         pads[m, 0:8, :] = jnp.full((8, 128), FAR, F32)
         pads[m, 40:48, :] = jnp.full((8, 128), FAR, F32)
-        pads[m, 8:40, :] = jnp.where(ok, column, FAR)
+        pads[m, 8:40, :] = jnp.where(ok, columns[m], FAR)
         ls[m * 8 : m * 8 + 8, :] = pads[m, pl.ds(2 * zt + 5, 8), :]
     lt = ls[...].T
     for number, (k, r) in enumerate(LINES):
@@ -90,7 +108,7 @@
                 for l, (k, r) in enumerate(line_sets(dz, dy)):
                     q, zl = (k + 1) // 2, (k + 1) % 2
                     unit = orbs[q, r, h].astype(F32)
-                    shift = (l * 32 - zl * 64 - xq * 32) % 128
+                    shift = (l * 32 - xq * 64 - zl * 32) % 128
                     if shift:
                         unit = pltpu.roll(unit, shift, 1)
                     orb = unit if orb is None else jnp.where(group == l, unit, orb)
@@ -187,24 +205,27 @@
     return trial
 
 
-def finish(trial, factor, ug):
+def pots_by_cells(trial):
     columns = []
     for zl in range(2):
         plane = jnp.concatenate([trial[2 * zl], trial[2 * zl + 1]], axis=0)
         columns.append(plane.T.astype(BF16))
+    return columns
+
+
+def gram_part(columns):
     gram = None
-    for zl in range(2):
-        ug[zl] = jnp.dot(factor[...], columns[zl], preferred_element_type=F32)
-        part = lax.dot_general(columns[zl], columns[zl], (((1,), (1,)), ((), ())), preferred_element_type=F32)
+    for part in columns:
+        part = lax.dot_general(part, part, (((1,), (1,)), ((), ())), preferred_element_type=F32)
         gram = part if gram is None else gram + part
-    ug[2] = gram * (1.0 / 131072.0)
+    return gram * (1.0 / 131072.0)
 
 
 NEIGHBOURS = [
-    (1, 0, 0, 2, 0, 2), (-1, 0, 0, 2, 0, 2), (0, 1, 0, 2, 0, 2), (0, -1, 0, 2, 0, 2),
-    (2, 0, 1, 1, 0, 2), (-2, 0, 0, 1, 0, 2), (0, 2, 0, 2, 1, 1), (0, -2, 0, 2, 0, 1),
     (1, 1, 1, 1, 0, 2), (1, -1, 1, 1, 0, 2), (-1, 1, 0, 1, 0, 2), (-1, -1, 0, 1, 0, 2),
     (1, 1, 0, 1, 1, 1), (1, -1, 0, 1, 0, 1), (-1, 1, 1, 1, 1, 1), (-1, -1, 1, 1, 0, 1),
+    (0, 2, 0, 2, 1, 1), (0, -2, 0, 2, 0, 1), (2, 0, 1, 1, 0, 2), (-2, 0, 0, 1, 0, 2),
+    (0, 1, 0, 2, 0, 2), (0, -1, 0, 2, 0, 2), (1, 0, 0, 2, 0, 2), (-1, 0, 0, 2, 0, 2),
 ]
 ORB_NEIGHBOURS = [
     (1, 0, 0, 2), (-1, 0, 0, 2), (0, 1, 0, 2), (0, -1, 0, 2), (2, 0, 0, 2), (-2, 0, 0, 2),
@@ -222,10 +243,10 @@
 )
 
 
-def kernel(pot, orb_in, energies, loc, factor, out, margins,
-           rows_in, recv, lines, own, halo, orbs, ug, back, parts, pads, ls, bl, wf, pf, sf, qb, coef, vf,
+def kernel(pot_far, orb_far, energies_far, loc_far, factor_far, out, margins,
+           orb, energies, columns, factor, orb_in, recv, lines, own, halo, orbs, gram, gram_back, ug, parts, pads, ls, bl, wf, pf, sf, qb, coef, vf,
            row_send, row_recv, move_send, move_recv, orb_send, orb_recv, halo_send, halo_recv,
-           back_send, back_recv, part_send, part_recv):
+           gram_send, gram_recv, back_send, back_recv, part_send, part_recv, load_sem):
     me, g = lax.axis_index("pot"), lax.axis_index("grid")
     zp, yt = tile_of(me)
     zt = g * 4 + zp
@@ -238,8 +259,25 @@
         for y, x, z, c in OTHERS:
             yield ys[y] + xs[x] + zs[z] + cs[c]
 
+    def cells_of(y, x, z, c):
+        across = ys[y] // 8 % 2
+        to_yt = ys[y] // 2 + xs[x] // 2 + across * (3 - xs[x])
+        to_plane = zs[z] // 16 + cs[c] * 2
+        return pot_far.at[0, pl.ds(to_plane, 2), pl.ds(pl.multiple_of(to_yt * 128, 128), 128)]
+
     def near(a, b):
         return place((zt + a + 16) % 16, (yt + b + 32) % 32)
+
+    loads = [
+        pltpu.make_async_copy(orb_far, orb, load_sem.at[0]),
+        pltpu.make_async_copy(energies_far, energies, load_sem.at[1]),
+        pltpu.make_async_copy(factor_far, factor, load_sem.at[2]),
+    ]
+    for m in range(5):
+        at = pl.multiple_of(jnp.clip(yt - 2 + m, 0, NPAIR - 1) * 128, 128)
+        loads.append(pltpu.make_async_copy(loc_far.at[:, pl.ds(at, 128)], columns.at[m], load_sem.at[3 + m]))
+    for load in loads:
+        load.start()
 
     barrier = pltpu.get_barrier_semaphore()
     for to in others():
@@ -249,11 +287,9 @@
     for a, b, *_ in ORB_NEIGHBOURS:
         pl.semaphore_signal(barrier, inc=1, device_id=near(a, b), device_id_type=MESH)
 
-    for z in range(8):
-        for y in range(32):
-            to = device_of(z // 2, y)
-            rows_in[z % 2, to : to + 1, :] = pot[0, z : z + 1, y * 128 : y * 128 + 128]
-    build_weights(zt, yt, loc, energies, pads, ls, bl, wf, sf)
+    choose, fold = pack_helpers()
+    loads[0].wait()
+    pack_orbitals(orb, choose, fold, orb_in)
     pl.semaphore_wait(barrier, len(OTHERS) + 3 + len(ORB_NEIGHBOURS))
 
     row, half = me // 2, me % 2
@@ -269,11 +305,15 @@
         pl.when(to != me)(move.start)
         pl.when(to == me)(pltpu.make_async_copy(orb_in.at[to_zp], target, move_recv.at[landing]).start)
 
-    for to in others():
+    for to, offsets in zip(others(), OTHERS):
         pltpu.make_async_remote_copy(
-            rows_in.at[:, to, :], recv.at[:, me, :], row_send, row_recv,
+            cells_of(*offsets), recv.at[:, me, :], row_send, row_recv,
             device_id=(to, g), device_id_type=MESH).start()
-    pltpu.make_async_copy(rows_in.at[:, me, :], recv.at[:, me, :], row_recv).start()
+    pltpu.make_async_copy(cells_of(0, 0, 0, 0), recv.at[:, me, :], row_recv).start()
+
+    for load in loads[1:]:
+        load.wait()
+    build_weights(zt, yt, columns, energies, pads, ls, bl, wf, sf)
 
     for yl in range(2):
         for h in range(2):
@@ -311,31 +351,36 @@
     for copy in copies:
         copy.wait_recv()
     place_lines(halo, False, vf)
-    finish(apply_stencil(vf, coef), factor, ug)
-
+    columns = pots_by_cells(apply_stencil(vf, coef))
+
+    gram[0] = gram_part(columns)
     for to in others():
         pltpu.make_async_remote_copy(
-            ug.at[:, to, :], back.at[:, me, :], back_send, back_recv,
+            gram.at[:, to, :], gram_back.at[:, me, :], gram_send, gram_recv,
             device_id=(to, g), device_id_type=MESH).start()
-    pltpu.make_async_copy(ug.at[:, me, :], back.at[:, me, :], back_recv).start()
-    for copy in orb_copies + copies:
-        copy.wait_send()
-    for to, move in moves:
-        pl.when(to != me)(move.wait_send)
-    pltpu.make_async_copy(rows_in.at[:, 0:127, :], rows_in.at[:, 0:127, :], row_send).wait()
-
-    pltpu.make_async_copy(back, back, back_recv).wait()
-    parts[0] = jnp.broadcast_to(jnp.sum(back[2], axis=0, keepdims=True), (8, 128))
+    pltpu.make_async_copy(gram.at[:, me, :], gram_back.at[:, me, :], gram_recv).start()
+    for zl in range(2):
+        ug[zl] = jnp.dot(factor[...], columns[zl], preferred_element_type=F32)
+    cells = out.at[0, pl.ds(zp * 2, 2), pl.ds(pl.multiple_of(yt * 128, 128), 128)]
+    for to in others():
+        pltpu.make_async_remote_copy(
+            ug.at[:, to, :], cells, back_send, back_recv, device_id=(to, g), device_id_type=MESH).start()
+    pltpu.make_async_copy(ug.at[:, me, :], cells, back_recv).start()
+
+    pltpu.make_async_copy(gram_back, gram_back, gram_recv).wait()
+    parts[0] = jnp.broadcast_to(jnp.sum(gram_back[0], axis=0, keepdims=True), (8, 128))
     part_copies = []
     for step in range(1, 4):
         part_copies.append(pltpu.make_async_remote_copy(
             parts.at[0], parts.at[4 - step], part_send.at[step - 1], part_recv.at[step - 1],
             device_id=(me, (g + step) % 4), device_id_type=MESH))
         part_copies[-1].start()
-    for z in range(8):
-        for y in range(32):
-            source = device_of(z // 2, y)
-            out[0, z : z + 1, y * 128 : y * 128 + 128] = back[z % 2, source : source + 1, :]
+    for copy in orb_copies + copies:
+        copy.wait_send()
+    for to, move in moves:
+        pl.when(to != me)(move.wait_send)
+    pltpu.make_async_copy(recv.at[:, 0:127, :], recv.at[:, 0:127, :], row_send).wait()
+
     for copy in part_copies:
         copy.wait()
     total = None
@@ -343,27 +388,34 @@
         part = parts[(slab - g + 4) % 4]
         total = part if total is None else total + part
     margins[...] = total[0:1]
+    pltpu.make_async_copy(out, out, back_recv).wait()
     pltpu.make_async_copy(ug.at[:, 0:127, :], ug.at[:, 0:127, :], back_send).wait()
+    pltpu.make_async_copy(gram.at[:, 0:127, :], gram.at[:, 0:127, :], gram_send).wait()
 
 
 def local(potentials, orbitals, energies, local_potential, inverse_factor):
-    packed = orbitals.reshape(32, 4, 2, 2, 16).transpose(1, 4, 2, 3, 0).reshape(4, 16, 128)
+    hbm = pl.BlockSpec(memory_space=pltpu.HBM)
     vmem = pl.BlockSpec(memory_space=pltpu.VMEM)
     dma = pltpu.SemaphoreType.DMA
     return pl.pallas_call(
         kernel,
         out_shape=(jax.ShapeDtypeStruct((1, 8, 4096), F32), jax.ShapeDtypeStruct((1, 128), F32)),
-        in_specs=[vmem] * 5,
-        out_specs=(vmem,) * 2,
+        in_specs=[hbm] * 5,
+        out_specs=(hbm, vmem),
         scratch_shapes=[
-            pltpu.VMEM((2, 128, 128), F32),
+            pltpu.VMEM((32, 8, 32), BF16),
+            pltpu.VMEM((1, 32), F32),
+            pltpu.VMEM((5, 32, 128), F32),
+            pltpu.VMEM((128, 128), BF16),
+            pltpu.VMEM((4, 16, 128), BF16),
             pltpu.VMEM((2, 128, 128), F32),
             pltpu.VMEM((2, 2, 64, 128), BF16),
             pltpu.VMEM((2, 2, 64, 128), F32),
             pltpu.VMEM((8, 8, 64, 128), BF16),
             pltpu.VMEM((5, 8, 2, 16, 128), BF16),
-            pltpu.VMEM((3, 128, 128), F32),
-            pltpu.VMEM((3, 128, 128), F32),
+            pltpu.VMEM((1, 128, 128), F32),
+            pltpu.VMEM((1, 128, 128), F32),
+            pltpu.VMEM((2, 128, 128), F32),
             pltpu.VMEM((4, 8, 128), F32),
             pltpu.VMEM((5, 48, 128), F32),
             pltpu.VMEM((128, 128), F32),
@@ -375,11 +427,11 @@
             pltpu.VMEM((COUNT * 64, 512), F32),
             pltpu.VMEM((len(LINES), 80, 128), F32),
             dma, dma, dma((4,)), dma((4,)), dma((12,)), dma((12,)), dma((16,)), dma((16,)),
-            dma, dma, dma((3,)), dma((3,)),
+            dma, dma, dma, dma, dma((3,)), dma((3,)), dma((8,)),
         ],
         compiler_params=pltpu.CompilerParams(
-            collective_id=0, has_side_effects=True, vmem_limit_bytes=48 * 1024 * 1024),
-    )(potentials, packed, energies.reshape(1, 32), local_potential, inverse_factor)
+            collective_id=0, has_side_effects=True, vmem_limit_bytes=58 * 1024 * 1024),
+    )(potentials, orbitals, energies.reshape(1, 32), local_potential, inverse_factor)
 
 
 def solution(mesh):

time: 49.4 us -> 47.9 us (0.970)
  local copies, waits for them, and re-layouts: 4.04 us -> 2.08 us
  Pallas kernels: 44.5 us -> 45 us
    unnamed x11 -> x4, local copies, waits for them, and re-layouts: 3.88 us -> 2.08 us
    pallas_call x1, Pallas kernels: 44.5 us -> 45 us  [local(): pl.pallas_call(kernel, out_shape=(jax.ShapeDtypeStruct((1, 8, 4096), F32)...]
where the time goes in v3:
time: 47.9 us; the launch traced here: 47.8 us
  Pallas kernels  45 us (94%)
  local copies, waits for them, and re-layouts  2.08 us (4%)
  between operations  0.65 us (1%)
    pallas_call x1, Pallas kernels, local(): pl.pallas_call(kernel, out_shape=(jax.ShapeDtypeStruct((1, 8, 4096), F32)...  45 us
    unnamed x4, local copies, waits for them, and re-layouts  2.08 us

profile of v3, /device:TPU:1, one launch (start us, length us, event | category | flops | bytes accessed | tf_op | source)
XLA Modules:
  0.0 47.8 jit_solution(1185024368727705216)
XLA Ops:
  0.6 45.0 %shard_map.68 = (f32[1,8,4096]{2,1,0:T(8,128)}, f32[1,128]{1,0:T(1,128)}) custom-call(f32[1,8,4096]{2,1,0:T(8,128)} %pot_far.1, bf16[32,8,32]{2,1,0:T(8,128)(2,1)} %orb_far.1, f32[1,32]{1,0:T(1,128)} %bitcast.1, f32[32,4096]{1,0:T(8,128)} %loc_far.1, bf16[128,128]{1,0:T(8,128)(2,1)} %factor_far.1), custom_call_target="tpu_custom_call" | custom-call | tf_op jit(solution)/shard_map/pallas_call | solution.py:400
  45.7 0.0 copy-start
  45.7 1.6 %copy.9 = f32[1,8,4096]{2,1,0:T(8,128)} copy(f32[1,8,4096]{2,1,0:T(8,128)} %get-tuple-element.4) | data formatting | bytes 262144
  47.2 0.0 copy-done
  47.2 0.5 %copy.10 = f32[1,128]{1,0:T(1,128)} copy(f32[1,128]{1,0:T(1,128)S(1)} %copy-done) | data formatting | bytes 1024
Async XLA Ops:
  45.7 1.6 %copy-start = (f32[1,128]{1,0:T(1,128)S(1)}, f32[1,128]{1,0:T(1,128)}, u32[]{:S(2)}) copy-start(f32[1,128]{1,0:T(1,128)} %get-tuple-element.5) | copy-start | bytes 1540

commit v4 on v3

--- a/solution.py
+++ b/solution.py
@@ -311,10 +311,6 @@
             device_id=(to, g), device_id_type=MESH).start()
     pltpu.make_async_copy(cells_of(0, 0, 0, 0), recv.at[:, me, :], row_recv).start()
 
-    for load in loads[1:]:
-        load.wait()
-    build_weights(zt, yt, columns, energies, pads, ls, bl, wf, sf)
-
     for yl in range(2):
         for h in range(2):
             landed = orbs.at[2, 3 + yl, h]
@@ -341,6 +337,10 @@
             lines.at[z0 : z0 + nz, y0 : y0 + ny], halo.at[zz : zz + nz, yy : yy + ny],
             halo_send.at[number], halo_recv.at[number], device_id=near(a, b), device_id_type=MESH))
         copies[-1].start()
+
+    for load in loads[1:]:
+        load.wait()
+    build_weights(zt, yt, columns, energies, pads, ls, bl, wf, sf)
 
     for copy in orb_copies:
         copy.wait_recv()

time: 47.9 us -> 47.9 us (level)
  no operation moved by 1% of the time
where the time goes in v4:
time: 47.9 us; the launch traced here: 47.8 us
  Pallas kernels  45 us (94%)
  local copies, waits for them, and re-layouts  2.08 us (4%)
  between operations  0.65 us (1%)
    pallas_call x1, Pallas kernels, local(): pl.pallas_call(kernel, out_shape=(jax.ShapeDtypeStruct((1, 8, 4096), F32)...  45 us
    unnamed x4, local copies, waits for them, and re-layouts  2.08 us

profile of v4, /device:TPU:1, one launch (start us, length us, event | category | flops | bytes accessed | tf_op | source)
XLA Modules:
  0.0 47.8 jit_solution(2518556672255010661)
XLA Ops:
  0.6 45.0 %shard_map.68 = (f32[1,8,4096]{2,1,0:T(8,128)}, f32[1,128]{1,0:T(1,128)}) custom-call(f32[1,8,4096]{2,1,0:T(8,128)} %pot_far.1, bf16[32,8,32]{2,1,0:T(8,128)(2,1)} %orb_far.1, f32[1,32]{1,0:T(1,128)} %bitcast.1, f32[32,4096]{1,0:T(8,128)} %loc_far.1, bf16[128,128]{1,0:T(8,128)(2,1)} %factor_far.1), custom_call_target="tpu_custom_call" | custom-call | tf_op jit(solution)/shard_map/pallas_call | solution.py:400
  45.7 0.0 copy-start
  45.7 1.6 %copy.9 = f32[1,8,4096]{2,1,0:T(8,128)} copy(f32[1,8,4096]{2,1,0:T(8,128)} %get-tuple-element.4) | data formatting | bytes 262144
  47.2 0.0 copy-done
  47.3 0.5 %copy.10 = f32[1,128]{1,0:T(1,128)} copy(f32[1,128]{1,0:T(1,128)S(1)} %copy-done) | data formatting | bytes 1024
Async XLA Ops:
  45.7 1.6 %copy-start = (f32[1,128]{1,0:T(1,128)S(1)}, f32[1,128]{1,0:T(1,128)}, u32[]{:S(2)}) copy-start(f32[1,128]{1,0:T(1,128)} %get-tuple-element.5) | copy-start | bytes 1540

commit v5 on v4

--- a/solution.py
+++ b/solution.py
@@ -193,13 +193,16 @@
         vf[number, 8:72, :] = source[k - 3, r - 3] if here else source[k, r].astype(F32)
 
 
-def apply_stencil(vf, coef):
+def apply_stencil(vf, coef, inside, start):
     trial = []
     for l in range(4):
         zl, yl = l // 2, l % 2
-        total = vf[LINE_INDEX[(3 + zl, 3 + yl)], 8:72, :]
+        total = start[l]
         for number, (dz, dy, dx) in enumerate(OFFSETS):
-            field = vf[LINE_INDEX[(3 + zl + dz, 3 + yl + dy)], 8 + dx : 72 + dx, :]
+            line = (3 + zl + dz, 3 + yl + dy)
+            if (3 <= line[0] <= 4 and 3 <= line[1] <= 4) != inside:
+                continue
+            field = vf[LINE_INDEX[line], 8 + dx : 72 + dx, :]
             total = total + coef[number * 64 : number * 64 + 64, l * 128 : l * 128 + 128] * field
         trial.append(total)
     return trial
@@ -348,10 +351,11 @@
     build_products(wf, pf, sf, qb)
     build_coefficients(qb, coef)
     place_lines(own, True, vf)
+    partial = apply_stencil(vf, coef, True, [own[l // 2, l % 2] for l in range(4)])
     for copy in copies:
         copy.wait_recv()
     place_lines(halo, False, vf)
-    columns = pots_by_cells(apply_stencil(vf, coef))
+    columns = pots_by_cells(apply_stencil(vf, coef, False, partial))
 
     gram[0] = gram_part(columns)
     for to in others():

time: 47.9 us -> 47.8 us (level)
  no operation moved by 1% of the time
where the time goes in v5:
time: 47.8 us; the launch traced here: 47.6 us
  Pallas kernels  44.9 us (94%)
  local copies, waits for them, and re-layouts  2.08 us (4%)
  between operations  0.65 us (1%)
    pallas_call x1, Pallas kernels, local(): pl.pallas_call(kernel, out_shape=(jax.ShapeDtypeStruct((1, 8, 4096), F32)...  44.9 us
    unnamed x4, local copies, waits for them, and re-layouts  2.08 us

profile of v5, /device:TPU:1, one launch (start us, length us, event | category | flops | bytes accessed | tf_op | source)
XLA Modules:
  0.0 47.6 jit_solution(3946937290159167019)
XLA Ops:
  0.6 44.9 %shard_map.68 = (f32[1,8,4096]{2,1,0:T(8,128)}, f32[1,128]{1,0:T(1,128)}) custom-call(f32[1,8,4096]{2,1,0:T(8,128)} %pot_far.1, bf16[32,8,32]{2,1,0:T(8,128)(2,1)} %orb_far.1, f32[1,32]{1,0:T(1,128)} %bitcast.1, f32[32,4096]{1,0:T(8,128)} %loc_far.1, bf16[128,128]{1,0:T(8,128)(2,1)} %factor_far.1), custom_call_target="tpu_custom_call" | custom-call | tf_op jit(solution)/shard_map/pallas_call | solution.py:404
  45.6 0.0 copy-start
  45.6 1.6 %copy.9 = f32[1,8,4096]{2,1,0:T(8,128)} copy(f32[1,8,4096]{2,1,0:T(8,128)} %get-tuple-element.4) | data formatting | bytes 262144
  47.1 0.0 copy-done
  47.1 0.5 %copy.10 = f32[1,128]{1,0:T(1,128)} copy(f32[1,128]{1,0:T(1,128)S(1)} %copy-done) | data formatting | bytes 1024
Async XLA Ops:
  45.6 1.6 %copy-start = (f32[1,128]{1,0:T(1,128)S(1)}, f32[1,128]{1,0:T(1,128)}, u32[]{:S(2)}) copy-start(f32[1,128]{1,0:T(1,128)} %get-tuple-element.5) | copy-start | bytes 1540
